TPU v7x, 256 devices: a whole 4x4x8 slice. The times are simulated.
256 devices in a mesh: row: 4 (over x_lo, core), col: 16 (over z, x_hi), layer: 4 (over y).
Axes of the slice: x: 4 (x_hi: 2, x_lo: 2; x = x_hi * 2 + x_lo), y: 4, z: 8, core: 2. Of those that a mesh axis runs over, the one named last changes fastest.
Arguments:
- left_values: float32 [4, 8192, 4096], P('layer', 'row', 'col'), may hold values from -6 to 6
- left_pattern: int32 [4, 64, 32], P('layer', 'row', 'col'), may hold values from 0 to 1, as said below
- right_values: float32 [4, 4096, 4096], P('layer', 'row', 'col'), may hold values from -0.046875 to 0.046875
- right_pattern: int32 [4, 32, 32], P('layer', 'row', 'col'), may hold values from 0 to 1, as said below
Outputs:
- product: float32 [8192, 4096], P(('row', 'layer'), 'col')
Inputs may be any that keep to these rules, and one draw needn't show every extreme that they name: `left_pattern`: 1 marks an occupied block, 0 an empty one. `right_pattern`: 1 marks an occupied block, 0 an empty one.
All inputs are finite; a program needn't handle non-finite values.
Results may differ from a plain program's by a relative error of at most 0.0001.
Values sent between devices are 32-bit elements; how exact they have to be, the bound alone decides.
No kernel may reach another device: no remote copies, remote signals or barrier semaphores. Data moves between devices by JAX's collectives and lax.ppermute only.
A program may use at most 128 MiB of HBM per device.

v0:
```python
import jax
import jax.numpy as jnp
from jax import lax
from jax.sharding import PartitionSpec as P

BS = 128


def spread(pattern, size):
    return jnp.repeat(jnp.repeat(pattern, size, axis=0), size, axis=1).astype(jnp.float32)


def body(left_values, left_pattern, right_values, right_pattern):
    left = left_values[0] * spread(left_pattern[0], BS)
    right = right_values[0] * spread(right_pattern[0], BS)
    right_slab = lax.all_gather(right, "row", axis=0, tiled=True)
    right_panel = lax.all_to_all(right_slab, "col", split_axis=0, concat_axis=1, tiled=True)
    terms = jnp.dot(
        left, right_panel, preferred_element_type=jnp.float32, precision=lax.Precision.HIGHEST
    )
    partial_value = lax.psum_scatter(terms, "col", scatter_dimension=1, tiled=True)
    return lax.psum_scatter(partial_value, "layer", scatter_dimension=0, tiled=True)


def solution(mesh):
    in_specs = (
        P("layer", "row", "col"),
        P("layer", "row", "col"),
        P("layer", "row", "col"),
        P("layer", "row", "col"),
    )
    out_specs = P(("row", "layer"), "col")
    return jax.shard_map(body, mesh=mesh, in_specs=in_specs, out_specs=out_specs, check_vma=False)
```

profile of v0, /device:TPU:56, one launch (start us, length us, event | category | flops | bytes accessed | tf_op | source)
XLA Modules:
  0.0 777.1 jit_solution(13230635650748036046)
XLA Ops:
  6.5 0.0 copy-start
  6.5 0.0 all-gather.2.cloned.1.call-start
  6.5 0.8 convert_bitcast_fusion
  7.3 0.1 copy.10
  7.4 1.2 broadcast_in_dim.15
  8.7 0.0 copy-done
  8.7 1.1 bitcast_multiply_fusion
  9.8 0.0 all-gather.2.cloned.1.call-update
  9.8 51.0 %all-gather.2.cloned.1.call-done = f32[4096,256]{1,0:T(8,128)} async-done(((f32[1024,256]{1,0:T(8,128)}), f32[4096,256]{1,0:T(8,128)}) %all-gather.2.cloned.1.call-update) | async-done | bytes 4194320 | tf_op jit(solution)/shard_map/all_gather | solution.py:16
  60.8 0.0 copy-start.1
  60.8 9.7 %all-to-all-start = ((f32[16,256,256]{2,1,0:T(8,128)}), f32[16,256,256]{2,1,0:T(8,128)}, u32[]{:S(2)}, u32[]{:S(2)}) async-start(f32[16,256,256]{2,1,0:T(8,128)} %bitcast.21), calls=%async_computation | async-start | bytes 8388608 | tf_op jit(solution)/shard_map/all_to_all | solution.py:17
  70.6 0.0 reduce-scatter.3.cloned.1.call-start
  70.6 0.0 copy-done.1
  70.7 0.1 copy.9
  70.7 0.1 broadcast_in_dim.12
  70.8 5.4 broadcast_in_dim.13
  76.3 2.9 convert_element_type.38
  79.2 87.9 %all-to-all-done = f32[16,256,256]{2,1,0:T(8,128)} async-done(((f32[16,256,256]{2,1,0:T(8,128)}), f32[16,256,256]{2,1,0:T(8,128)}, u32[]{:S(2)}, u32[]{:S(2)}) %all-to-all-start) | async-done | bytes 4194336 | tf_op jit(solution)/shard_map/all_to_all | solution.py:17
  167.1 5.4 copy.11
  172.5 32.7 %fusion = f32[2048,4096]{1,0:T(8,128)} fusion(f32[256,4096]{0,1:T(8,128)} %bitcast.18, f32[1,2048,256]{2,1,0:T(8,128)} %param.4, f32[1,2048,256]{2,1,0:T(8,128)S(1)} %convert_element_type.38), kind=kOutput, calls=%fused_computation | convolution fusion | flops 25770328064 | bytes 41943040 | tf_op jit(solution)/shard_map/dot_general | solution.py:18
  205.2 0.0 reduce-scatter.3.cloned.1.call-update
  205.2 0.0 reduce-scatter.5.cloned.1.call-start
  205.3 532.6 %reduce-scatter.3.cloned.1.call-done = f32[2048,256]{1,0:T(8,128)} async-done(((f32[2048,4096]{1,0:T(8,128)}), f32[2048,256]{1,0:T(8,128)}) %reduce-scatter.3.cloned.1.call-update) | async-done | bytes 2097168 | tf_op jit(solution)/shard_map/reduce_scatter | solution.py:21
  737.9 0.0 reduce-scatter.5.cloned.1.call-update
  737.9 32.6 %reduce-scatter.5.cloned.1.call-done = f32[512,256]{1,0:T(8,128)} async-done(((f32[2048,256]{1,0:T(8,128)}), f32[512,256]{1,0:T(8,128)}) %reduce-scatter.5.cloned.1.call-update) | async-done | bytes 524304 | tf_op jit(solution)/shard_map/reduce_scatter | solution.py:22
  (2 shorter events, 0.0 us)
Async XLA Ops:
  6.5 2.1 copy-start
  6.5 54.3 %all-gather.2.cloned.1.call-start = ((), (), s32[]{:S(2)}) async-start(), calls=%async_computation.3 | async-start | bytes 5242880 | tf_op jit(solution)/shard_map/all_gather | solution.py:16
  60.8 9.8 %copy-start.1 = (s32[1,16,2]{1,2,0:T(2,128)S(1)}, s32[1,16,2]{1,2,0:T(2,128)}, u32[]{:S(2)}) copy-start(s32[1,16,2]{1,2,0:T(2,128)} %param.5) | copy-start | bytes 388
  60.8 106.2 %all-to-all-start = ((f32[16,256,256]{2,1,0:T(8,128)}), f32[16,256,256]{2,1,0:T(8,128)}, u32[]{:S(2)}, u32[]{:S(2)}) async-start(f32[16,256,256]{2,1,0:T(8,128)} %bitcast.21), calls=%async_computation | async-start | bytes 8388608 | tf_op jit(solution)/shard_map/all_to_all | solution.py:17
  70.6 667.3 %reduce-scatter.3.cloned.1.call-start = ((), (), s32[]{:S(2)}) async-start(), calls=%async_computation.4 | async-start | bytes 35651584 | tf_op jit(solution)/shard_map/reduce_scatter | solution.py:21
  205.2 565.3 %reduce-scatter.5.cloned.1.call-start = ((), (), s32[]{:S(2)}) async-start(), calls=%async_computation.5 | async-start | bytes 2621440 | tf_op jit(solution)/shard_map/reduce_scatter | solution.py:22
Sparse Core Ops, SparseCore 0:
  9.9 50.8 all-gather.1
  205.3 532.4 reduce-scatter.2
  740.6 29.8 reduce-scatter.4
where the time goes:
time: 781 us; the launch traced here: 777 us
  waiting for transfers between devices  704 us (90%)
  matrix products  32.7 us (4%)
  local copies, waits for them, and re-layouts  15.3 us (2%)
  between operations  13.2 us (2%)
  starting transfers between devices  9.83 us (1%)
    reduce_scatter x1, waiting for transfers between devices, body(): lax.psum_scatter(terms, 'col', scatter_dimension=1, tiled=True)  533 us
    all_to_all x1, waiting for transfers between devices, body(): lax.all_to_all(right_slab, 'col', split_axis=0, concat_axis=1, tiled=True)  87.9 us
    all_gather x1, waiting for transfers between devices, body(): right_slab = lax.all_gather(right, 'row', axis=0, tiled=True)  51 us
    dot_general x1, matrix products, body(): jnp.dot(left, right_panel, preferred_element_type=jnp.float32, precision=...  32.7 us
    reduce_scatter x1, waiting for transfers between devices, body(): lax.psum_scatter(partial_value, 'layer', scatter_dimension=0, tiled=True)  32.6 us
  transfers between devices with their start and end apart: 4, of which 4 were waited for; matrix products, arithmetic and copies ran while one was open for 1% of the time, Pallas kernels for 0%

commit v1 on v0

v1 whole, which is shorter than its diff:
```python
import jax
import jax.numpy as jnp
from jax import lax
from jax.experimental import pallas as pl
from jax.experimental.pallas import tpu as pltpu
from jax.sharding import Mesh, PartitionSpec as P

BS = 128
F32 = jnp.float32
BF16 = jnp.bfloat16
VMEM_BYTES = 48 * 1024 * 1024


def mask_left_kernel(pattern_ref, values_ref, out_ref):
    at = pl.program_id(0)
    for i in range(2):
        for j in range(2):
            rows, columns = slice(i * BS, (i + 1) * BS), slice(j * BS, (j + 1) * BS)
            keep = pattern_ref[2 * at + i, j].astype(F32)
            out_ref[rows, columns] = values_ref[rows, columns] * keep


def mask_left(values, pattern):
    rows = values.shape[0]
    return pl.pallas_call(
        mask_left_kernel,
        grid=(rows // 256,),
        in_specs=[
            pl.BlockSpec(memory_space=pltpu.SMEM),
            pl.BlockSpec((256, 256), lambda i: (i, 0)),
        ],
        out_specs=pl.BlockSpec((256, 256), lambda i: (i, 0)),
        out_shape=jax.ShapeDtypeStruct(values.shape, F32),
        cost_estimate=pl.CostEstimate(flops=values.size, bytes_accessed=8 * values.size, transcendentals=0),
    )(pattern, values)


def mask_right_kernel(pattern_ref, values_ref, out_ref):
    at = pl.program_id(0)
    for h in range(4):
        for j in range(2):
            columns = slice(j * BS, (j + 1) * BS)
            keep = pattern_ref[2 * at + h // 2, j].astype(F32)
            out_ref[h, 0, :, columns] = values_ref[h * 64 : (h + 1) * 64, columns] * keep


def mask_right(values, pattern):
    return pl.pallas_call(
        mask_right_kernel,
        grid=(4,),
        in_specs=[
            pl.BlockSpec(memory_space=pltpu.SMEM),
            pl.BlockSpec((256, 256), lambda i: (i, 0)),
        ],
        out_specs=pl.BlockSpec((4, 1, 64, 256), lambda i: (0, i, 0, 0)),
        out_shape=jax.ShapeDtypeStruct((4, 4, 64, 256), F32),
        cost_estimate=pl.CostEstimate(flops=values.size, bytes_accessed=8 * values.size, transcendentals=0),
    )(pattern, values)


def prepare_kernel(where_ref, b0_ref, b1_ref, b2_ref, b3_ref, high_ref, low_ref):
    xh = where_ref[8]
    for i, ref in enumerate((b0_ref, b1_ref, b2_ref, b3_ref)):
        rows = pl.ds(pl.multiple_of(where_ref[4 + i] * 64, 64), 64)
        for z0 in range(2):
            for near in range(2):
                block = ref[2 * z0 + lax.bitwise_xor(xh, jnp.int32(near))]
                high = block.astype(BF16)
                low = (block - high.astype(F32)).astype(BF16)
                columns = slice(z0 * 512 + near * 256, z0 * 512 + near * 256 + 256)
                high_ref[rows, columns] = high
                low_ref[rows, columns] = low


def prepare(where, parts):
    spec = pl.BlockSpec((4, 64, 256), lambda t, s: (s[t], 0, 0))
    out = pl.BlockSpec((256, 1024), lambda t, s: (t, 0))
    return pl.pallas_call(
        prepare_kernel,
        grid_spec=pltpu.PrefetchScalarGridSpec(
            num_scalar_prefetch=1, grid=(4,), in_specs=[spec] * 4, out_specs=[out] * 2
        ),
        out_shape=[jax.ShapeDtypeStruct((1024, 1024), BF16)] * 2,
        cost_estimate=pl.CostEstimate(flops=3 << 20, bytes_accessed=8 << 20, transcendentals=0),
    )(where, *parts)


def split(block):
    high = block.astype(BF16)
    return high, (block - high.astype(F32)).astype(BF16)


def product_kernel(a0_ref, a1_ref, a2_ref, a3_ref, high_ref, low_ref, *out_refs):
    pieces = [split(ref[...]) for ref in (a0_ref, a1_ref, a2_ref, a3_ref)]
    high = jnp.concatenate([p[0] for p in pieces], axis=1)
    low = jnp.concatenate([p[1] for p in pieces], axis=1)
    for z0 in range(2):
        columns = slice(z0 * 512, (z0 + 1) * 512)
        terms = jnp.dot(low, high_ref[:, columns], preferred_element_type=F32)
        terms += jnp.dot(high, low_ref[:, columns], preferred_element_type=F32)
        terms += jnp.dot(high, high_ref[:, columns], preferred_element_type=F32)
        if len(out_refs) == 1:
            out_refs[0][z0] = terms
        else:
            out_refs[0][z0] = terms[:, :256]
            out_refs[1][z0] = terms[:, 256:]


def partial_product(blocks, high, low, half, n_out):
    width = 512 // n_out
    return pl.pallas_call(
        product_kernel,
        grid=(4,),
        in_specs=[pl.BlockSpec((256, 256), lambda i: (2 * i + half, 0))] * 4
        + [pl.BlockSpec((1024, 1024), lambda i: (0, 0))] * 2,
        out_specs=[pl.BlockSpec((2, 256, width), lambda i: (i, 0, 0))] * n_out,
        out_shape=[jax.ShapeDtypeStruct((8, 256, width), F32)] * n_out,
        compiler_params=pltpu.CompilerParams(vmem_limit_bytes=VMEM_BYTES),
        cost_estimate=pl.CostEstimate(flops=6 << 30, bytes_accessed=12 << 20, transcendentals=0),
    )(*blocks, high, low)


def swap(value, axis):
    return lax.ppermute(value, axis, [(0, 1), (1, 0)])


def body(left_values, left_pattern, right_values, right_pattern):
    xl, core, xh, y = (lax.axis_index(n) for n in ("xl", "core", "xh", "y"))
    turn = 1 - 2 * core
    where = jnp.stack(
        [(y - turn * t + 4) % 4 for t in range(4)]
        + [2 * xl + core, 2 * (1 - xl) + core, 2 * xl + 1 - core, 2 * (1 - xl) + 1 - core, xh]
    ).astype(jnp.int32)

    left = mask_left(left_values[0], left_pattern[0])
    right = mask_right(right_values[0], right_pattern[0])

    ring = [(c * 4 + i, c * 4 + (i + 1 - 2 * c) % 4) for c in range(2) for i in range(4)]
    blocks = [left]
    for _ in range(3):
        blocks.append(lax.ppermute(blocks[-1], ("core", "y"), ring))

    right = right.reshape(16, 64, 256)
    right = lax.all_to_all(right, ("xl", "core"), split_axis=0, concat_axis=0, tiled=True)
    right = lax.all_to_all(right, ("z", "xh"), split_axis=0, concat_axis=0, tiled=True)
    right = lax.all_to_all(right, "y", split_axis=0, concat_axis=0, tiled=True)
    right_far = swap(right, "xl")
    parts = (right, right_far, swap(right, "core"), swap(right_far, "core"))
    high, low = prepare(where, parts)

    keep, send = partial_product(blocks, high, low, 1, 2)
    (both,) = partial_product(blocks, high, low, 0, 1)
    got = swap(send, "xh")
    second = lax.psum_scatter(keep + got, "z", scatter_dimension=0, tiled=True)[0]
    first = lax.psum_scatter(both, "z", scatter_dimension=0, tiled=True)[0]
    first = first[:, :256] + swap(first[:, 256:], "xh")

    turned = [
        ((2 * b + z0) * 4 + a, (2 * a + z0) * 4 + b) for a in range(4) for b in range(4) for z0 in range(2)
    ]
    mine = jnp.concatenate([first, second], axis=0)
    return lax.ppermute(mine, ("z", "y"), turned)


def solution(mesh):
    fine = Mesh(mesh.devices.reshape(2, 2, 8, 2, 4), ("xl", "core", "z", "xh", "y"))
    spec = P("y", ("xl", "core"), ("z", "xh"))
    return jax.shard_map(
        body,
        mesh=fine,
        in_specs=(spec,) * 4,
        out_specs=P(("xl", "core", "y"), ("z", "xh")),
        check_vma=False,
    )
```

time: 781 us -> 285 us (0.36)
  waiting for transfers between devices: 704 us -> 169 us
  blocking collectives: 0 us -> 36.7 us
  Pallas kernels: 0 us -> 35.2 us
  matrix products: 32.7 us -> 0 us
  starting transfers between devices: 9.83 us -> 20.1 us
  local copies, waits for them, and re-layouts: 15.3 us -> 5.96 us
    reduce_scatter x2, waiting for transfers between devices: 565 us -> 29.6 us  [the longest x1 29.5 us: body(): lax.psum_scatter(keep + got, 'z', scatter_dimension=0, tiled=True)[0]]
    ppermute x0 -> x9, waiting for transfers between devices: none -> 114 us  [the longest x5 80.3 us: swap(): return lax.ppermute(value, axis, [(0, 1), (1, 0)])]
    all_to_all x1, waiting for transfers between devices: 87.9 us -> 25.1 us  [body(): lax.all_to_all(right, ('z', 'xh'), split_axis=0, concat_axis=0, tiled=True)]
    all_gather x1 -> x0, waiting for transfers between devices: 51 us -> none  [body(): right_slab = lax.all_gather(right, 'row', axis=0, tiled=True)]
    all_to_all x0 -> x2, blocking collectives: none -> 36.7 us  [the longest x1 18.8 us: body(): lax.all_to_all(right, ('xl', 'core'), split_axis=0, concat_axis=0, tiled=...]
    pallas_call x0 -> x5, Pallas kernels: none -> 35.2 us  [the longest x2 20.6 us: partial_product(): pl.pallas_call(product_kernel, grid=(4,), in_specs=[pl.BlockSpec((256, 25...]
    dot_general x1 -> x0, matrix products: 32.7 us -> none  [body(): jnp.dot(left, right_panel, preferred_element_type=jnp.float32, precision=...]
    ppermute x0 -> x9, starting transfers between devices: none -> 9.01 us  [the longest x3 4.05 us: body(): blocks.append(lax.ppermute(blocks[-1], ('core', 'y'), ring))]
  transfers between devices with their start and end apart: 4 -> 12, of which waited for: 4 -> 7; matrix products, arithmetic and copies ran while one was open for 1% -> 2% of each run, Pallas kernels for 0% -> 7%
where the time goes in v1:
time: 285 us; the launch traced here: 284 us
  waiting for transfers between devices  169 us (59%)
  blocking collectives  36.7 us (13%)
  Pallas kernels  35.2 us (12%)
  starting transfers between devices  20.1 us (7%)
  between operations  13.5 us (5%)
  local copies, waits for them, and re-layouts  5.96 us (2%)
  other arithmetic  3.62 us (1%)
    ppermute x5, waiting for transfers between devices, swap(): return lax.ppermute(value, axis, [(0, 1), (1, 0)])  80.3 us
    ppermute x1, waiting for transfers between devices, body(): return lax.ppermute(mine, ('z', 'y'), turned)  34.1 us
    reduce_scatter x1, waiting for transfers between devices, body(): lax.psum_scatter(keep + got, 'z', scatter_dimension=0, tiled=True)[0]  29.5 us
    all_to_all x1, waiting for transfers between devices, body(): lax.all_to_all(right, ('z', 'xh'), split_axis=0, concat_axis=0, tiled=True)  25.1 us
    pallas_call x2, Pallas kernels, partial_product(): pl.pallas_call(product_kernel, grid=(4,), in_specs=[pl.BlockSpec((256, 25...  20.6 us
    all_to_all x1, blocking collectives, body(): lax.all_to_all(right, ('xl', 'core'), split_axis=0, concat_axis=0, tiled=...  18.8 us
    all_to_all x1, blocking collectives, body(): right = lax.all_to_all(right, 'y', split_axis=0, concat_axis=0, tiled=True)  17.9 us
    all_to_all x1, starting transfers between devices, body(): lax.all_to_all(right, ('z', 'xh'), split_axis=0, concat_axis=0, tiled=True)  11 us
  transfers between devices with their start and end apart: 12, of which 7 were waited for; matrix products, arithmetic and copies ran while one was open for 2% of the time, Pallas kernels for 7%

profile of v1, /device:TPU:56, one launch (start us, length us, event | category | flops | bytes accessed | tf_op | source)
XLA Modules:
  0.0 284.3 jit_solution(6637869246680674018)
XLA Ops:
  6.5 1.4 copy.5.pattern_ref
  7.9 0.0 copy-start.4
  7.9 5.7 %shard_map.46.a0_ref = f32[2048,256]{1,0:T(8,128)} custom-call(s32[16,2]{1,0:T(8,128)} %copy.5.pattern_ref, f32[2048,256]{1,0:T(8,128)} %bitcast.17), custom_call_target="tpu_custom_call" | custom-call | flops 524288 | bytes 4194304 | tf_op jit(solution)/shard_map/pallas_call | solution.py:25
  13.6 0.2 collective-permute-start
  13.9 0.0 copy-done.4
  13.9 0.7 copy.6.pattern_ref
  14.5 3.4 %shard_map.47 = f32[4,4,64,256]{3,2,1,0:T(8,128)} custom-call(s32[8,2]{1,0:T(8,128)} %copy.6.pattern_ref, f32[1024,256]{1,0:T(8,128)} %bitcast.18), custom_call_target="tpu_custom_call" | custom-call | flops 262144 | bytes 2097152 | tf_op jit(solution)/shard_map/pallas_call | solution.py:48
  18.0 18.8 %all_to_all.15 = f32[16,64,256]{2,1,0:T(8,128)} all-to-all(f32[16,64,256]{2,1,0:T(8,128)} %bitcast.16), channel_id=1, replica_groups=mesh['xl'=2,'core'=2,'z'=8,'xh'=2,'y'=4] {'xl','core'}, dimensions={0} | all-to-all | bytes 2097152 | tf_op jit(solution)/shard_map/all_to_all | solution.py:144
  36.7 11.0 %all-to-all-start.1 = ((f32[16,64,256]{2,1,0:T(8,128)}), f32[16,64,256]{2,1,0:T(8,128)}, u32[]{:S(2)}, u32[]{:S(2)}) async-start(f32[16,64,256]{2,1,0:T(8,128)} %all_to_all.15), calls=%async_computation.1 | async-start | bytes 2097152 | tf_op jit(solution)/shard_map/all_to_all | solution.py:145
  47.8 0.0 reduce-scatter.3.cloned.1.call-start
  47.8 0.0 collective-permute-done.a1_ref
  47.8 0.0 copy-start.1
  47.8 1.7 collective-permute-start.1
  49.5 25.1 %all-to-all-done.1 = f32[16,64,256]{2,1,0:T(8,128)} async-done(((f32[16,64,256]{2,1,0:T(8,128)}), f32[16,64,256]{2,1,0:T(8,128)}, u32[]{:S(2)}, u32[]{:S(2)}) %all-to-all-start.1) | async-done | bytes 1048608 | tf_op jit(solution)/shard_map/all_to_all | solution.py:145
  74.6 17.9 %all_to_all.16.b0_ref = f32[16,64,256]{2,1,0:T(8,128)S(1)} all-to-all(f32[16,64,256]{2,1,0:T(8,128)} %all-to-all-done.1), channel_id=1, replica_groups=mesh['xl'=2,'core'=2,'z'=8,'xh'=2,'y'=4] {'y'}, dimensions={0} | all-to-all | bytes 2097152 | tf_op jit(solution)/shard_map/all_to_all | solution.py:146
  92.5 0.0 copy-start.3
  92.5 0.0 collective-permute-start.3
  92.5 0.0 collective-permute-done.1.a2_ref
  92.5 2.1 collective-permute-start.2
  94.7 0.0 collective-permute-start.4
  94.7 20.8 %collective-permute-done.3.b1_ref = f32[16,64,256]{2,1,0:T(8,128)} collective-permute-done((f32[16,64,256]{2,1,0:T(8,128)S(1)}, f32[16,64,256]{2,1,0:T(8,128)}, u32[]{:S(2)}, u32[]{:S(2)}) %collective-permute-start.3) | collective-permute-done | bytes 1048608 | tf_op jit(solution)/shard_map/ppermute | solution.py:124
  115.4 0.0 collective-permute-start.5
  115.5 0.0 copy-done.1
  115.5 0.6 stack.39.where_ref
  116.0 0.0 copy-start
  116.0 0.0 collective-permute-done.4.b2_ref
  116.0 2.4 collective-permute-done.5.b3_ref
  118.5 0.0 copy-done.3
  118.5 5.5 %shard_map.48 = (bf16[1024,1024]{1,0:T(8,128)(2,1)}, bf16[1024,1024]{1,0:T(8,128)(2,1)}) custom-call(s32[9]{0:T(128)} %stack.39.where_ref, f32[16,64,256]{2,1,0:T(8,128)} %copy-done.3, f32[16,64,256]{2,1,0:T(8,128)} %collective-permute-done.3.b1_ref, f32[16,64,256]{2,1,0:T(8,128)} %collective-permute-done.4.b2_ref, f32[16,64,256]{2,1,0:T(8,128)} %collective-permute-done.5.b3_ref), custom_call_target="tpu_custom_call" | custom-call | flops 3145728 | bytes 8388608 | tf_op jit(solution)/shard_map/pallas_call | solution.py:78
  123.9 0.0 collective-permute-done.2.a3_ref
  124.0 0.0 copy-done
  124.0 0.0 copy-start.2
  124.0 1.6 copy-done.2
  125.5 10.6 %shard_map.49 = f32[8,256,512]{2,1,0:T(8,128)} custom-call(f32[2048,256]{1,0:T(8,128)S(1)} %copy-done, f32[2048,256]{1,0:T(8,128)S(1)} %copy-done.2, f32[2048,256]{1,0:T(8,128)} %collective-permute-done.1.a2_ref, f32[2048,256]{1,0:T(8,128)} %collective-permute-done.2.a3_ref, bf16[1024,1024]{1,0:T(8,128)(2,1)} %get-tuple-element.9.high_ref, ...), custom_call_target="tpu_custom_call" | custom-call | flops 6442450944 | bytes 12582912 | tf_op jit(solution)/shard_map/pallas_call | solution.py:111
  136.2 0.0 reduce-scatter.3.cloned.1.call-update
  136.2 0.0 reduce-scatter.5.cloned.1.call-start
  136.3 9.9 %shard_map.50 = (f32[8,256,256]{2,1,0:T(8,128)S(1)}, f32[8,256,256]{2,1,0:T(8,128)S(1)}) custom-call(f32[2048,256]{1,0:T(8,128)} %shard_map.46.a0_ref, f32[2048,256]{1,0:T(8,128)} %copy-done.1, f32[2048,256]{1,0:T(8,128)} %collective-permute-done.1.a2_ref, f32[2048,256]{1,0:T(8,128)} %collective-permute-done.2.a3_ref, ...), custom_call_target="tpu_custom_call" | custom-call | flops 6442450944 | bytes 12582912 | tf_op jit(solution)/shard_map/pallas_call | solution.py:111
  146.2 0.6 collective-permute-start.7
  146.8 48.6 %collective-permute-done.7 = f32[8,256,256]{2,1,0:T(8,128)S(1)} collective-permute-done((f32[8,256,256]{2,1,0:T(8,128)S(1)}, f32[8,256,256]{2,1,0:T(8,128)S(1)}, u32[]{:S(2)}, u32[]{:S(2)}) %collective-permute-start.7) | collective-permute-done | bytes 2097184 | tf_op jit(solution)/shard_map/ppermute | solution.py:124
  195.5 1.6 add.60
  197.1 0.0 reduce-scatter.5.cloned.1.call-update
  197.1 0.0 reduce-scatter.3.cloned.1.call-done
  197.1 1.0 slice.9
  198.1 0.6 collective-permute-start.6
  198.7 8.5 %collective-permute-done.6 = f32[256,256]{1,0:T(8,128)S(1)} collective-permute-done((f32[256,256]{1,0:T(8,128)S(1)}, f32[256,256]{1,0:T(8,128)S(1)}, u32[]{:S(2)}, u32[]{:S(2)}) %collective-permute-start.6) | collective-permute-done | bytes 262176 | tf_op jit(solution)/shard_map/ppermute | solution.py:124
  207.2 1.0 slice_add_fusion
  208.2 29.5 %reduce-scatter.5.cloned.1.call-done = f32[1,256,256]{2,1,0:T(8,128)} async-done(((f32[8,256,256]{2,1,0:T(8,128)}), f32[1,256,256]{2,1,0:T(8,128)}) %reduce-scatter.5.cloned.1.call-update) | async-done | bytes 262160 | tf_op jit(solution)/shard_map/reduce_scatter | solution.py:154
  237.8 1.0 pad_maximum_fusion
  238.8 3.7 %collective-permute-start.8 = (f32[512,256]{1,0:T(8,128)S(1)}, f32[512,256]{1,0:T(8,128)S(1)}, u32[]{:S(2)}, u32[]{:S(2)}) collective-permute-start(f32[512,256]{1,0:T(8,128)S(1)} %pad_maximum_fusion), channel_id=1, source_target_pairs={{0,0},{8,8},{16,1},{24,9},{32,2},{40,10},{48,3},{56,11},{1,16},{9,... | collective-permute-start | bytes 1572872 | tf_op jit(solution)/shard_map/ppermute | solution.py:162
  242.5 34.1 %collective-permute-done.8 = f32[512,256]{1,0:T(8,128)S(1)} collective-permute-done((f32[512,256]{1,0:T(8,128)S(1)}, f32[512,256]{1,0:T(8,128)S(1)}, u32[]{:S(2)}, u32[]{:S(2)}) %collective-permute-start.8) | collective-permute-done | bytes 524320 | tf_op jit(solution)/shard_map/ppermute | solution.py:162
  276.6 0.8 copy.8
Async XLA Ops:
  7.9 6.0 %copy-start.4 = (s32[1,8,2]{1,2,0:T(2,128)S(1)}, s32[1,8,2]{1,2,0:T(2,128)}, u32[]{:S(2)}) copy-start(s32[1,8,2]{1,2,0:T(2,128)} %param.7) | copy-start | bytes 196
  13.6 34.2 %collective-permute-start = (f32[2048,256]{1,0:T(8,128)}, f32[2048,256]{1,0:T(8,128)S(1)}, u32[]{:S(2)}, u32[]{:S(2)}) collective-permute-start(f32[2048,256]{1,0:T(8,128)} %shard_map.46.a0_ref), channel_id=1, source_target_pairs={{0,1},{1,2},{2,3},{3,0},{64,67},{65,64},{66,65},{67,66},{4,5},{5,6... | collective-permute-start | bytes 6291464 | tf_op jit(solution)/shard_map/ppermute | solution.py:141
  36.7 37.9 %all-to-all-start.1 = ((f32[16,64,256]{2,1,0:T(8,128)}), f32[16,64,256]{2,1,0:T(8,128)}, u32[]{:S(2)}, u32[]{:S(2)}) async-start(f32[16,64,256]{2,1,0:T(8,128)} %all_to_all.15), calls=%async_computation.1 | async-start | bytes 2097152 | tf_op jit(solution)/shard_map/all_to_all | solution.py:145
  47.8 149.4 %reduce-scatter.3.cloned.1.call-start = ((), (), s32[]{:S(2)}) async-start(), calls=%async_computation.5 | async-start | bytes 4718592 | tf_op jit(solution)/shard_map/reduce_scatter | solution.py:155
  47.8 67.6 %copy-start.1 = (f32[2048,256]{1,0:T(8,128)}, f32[2048,256]{1,0:T(8,128)S(1)}, u32[]{:S(2)}) copy-start(f32[2048,256]{1,0:T(8,128)S(1)} %collective-permute-done.a1_ref) | copy-start | bytes 6291460
  47.8 44.7 %collective-permute-start.1 = (f32[2048,256]{1,0:T(8,128)S(1)}, f32[2048,256]{1,0:T(8,128)}, u32[]{:S(2)}, u32[]{:S(2)}) collective-permute-start(f32[2048,256]{1,0:T(8,128)S(1)} %collective-permute-done.a1_ref), channel_id=1, source_target_pairs={{0,1},{1,2},{2,3},{3,0},{64,67},{65,64},{66,65},{67,66},{4,5},{5,6... | collective-permute-start | bytes 6291464 | tf_op jit(solution)/shard_map/ppermute | solution.py:141
  92.5 26.0 %copy-start.3 = (f32[16,64,256]{2,1,0:T(8,128)}, f32[16,64,256]{2,1,0:T(8,128)S(1)}, u32[]{:S(2)}) copy-start(f32[16,64,256]{2,1,0:T(8,128)S(1)} %all_to_all.16.b0_ref) | copy-start | bytes 3145732
  92.5 22.9 %collective-permute-start.3 = (f32[16,64,256]{2,1,0:T(8,128)S(1)}, f32[16,64,256]{2,1,0:T(8,128)}, u32[]{:S(2)}, u32[]{:S(2)}) collective-permute-start(f32[16,64,256]{2,1,0:T(8,128)S(1)} %all_to_all.16.b0_ref), channel_id=1, source_target_pairs={{0,128},{128,0},{1,129},{129,1},{2,130},{130,2},{3,131},{131,3},{4... | collective-permute-start | bytes 3145736 | tf_op jit(solution)/shard_map/ppermute | solution.py:124
  92.5 31.4 %collective-permute-start.2 = (f32[2048,256]{1,0:T(8,128)}, f32[2048,256]{1,0:T(8,128)}, u32[]{:S(2)}, u32[]{:S(2)}) collective-permute-start(f32[2048,256]{1,0:T(8,128)} %collective-permute-done.1.a2_ref), channel_id=1, source_target_pairs={{0,1},{1,2},{2,3},{3,0},{64,67},{65,64},{66,65},{67,66},{4,5},{5,6... | collective-permute-start | bytes 6291464 | tf_op jit(solution)/shard_map/ppermute | solution.py:141
  94.7 21.4 %collective-permute-start.4 = (f32[16,64,256]{2,1,0:T(8,128)S(1)}, f32[16,64,256]{2,1,0:T(8,128)}, u32[]{:S(2)}, u32[]{:S(2)}) collective-permute-start(f32[16,64,256]{2,1,0:T(8,128)S(1)} %all_to_all.16.b0_ref), channel_id=1, source_target_pairs={{0,64},{64,0},{1,65},{65,1},{2,66},{66,2},{3,67},{67,3},{4,68},{68... | collective-permute-start | bytes 3145736 | tf_op jit(solution)/shard_map/ppermute | solution.py:124
  115.4 3.0 %collective-permute-start.5 = (f32[16,64,256]{2,1,0:T(8,128)}, f32[16,64,256]{2,1,0:T(8,128)}, u32[]{:S(2)}, u32[]{:S(2)}) collective-permute-start(f32[16,64,256]{2,1,0:T(8,128)} %collective-permute-done.3.b1_ref), channel_id=1, source_target_pairs={{0,64},{64,0},{1,65},{65,1},{2,66},{66,2},{3,67},{67,3},{4,68},{68... | collective-permute-start | bytes 3145736 | tf_op jit(solution)/shard_map/ppermute | solution.py:124
  116.0 7.9 %copy-start = (f32[2048,256]{1,0:T(8,128)S(1)}, f32[2048,256]{1,0:T(8,128)}, u32[]{:S(2)}) copy-start(f32[2048,256]{1,0:T(8,128)} %shard_map.46.a0_ref) | copy-start | bytes 6291460
  124.0 1.6 copy-start.2
  136.2 101.6 %reduce-scatter.5.cloned.1.call-start = ((), (), s32[]{:S(2)}) async-start(), calls=%async_computation.6 | async-start | bytes 2359296 | tf_op jit(solution)/shard_map/reduce_scatter | solution.py:154
  146.2 49.3 %collective-permute-start.7 = (f32[8,256,256]{2,1,0:T(8,128)S(1)}, f32[8,256,256]{2,1,0:T(8,128)S(1)}, u32[]{:S(2)}, u32[]{:S(2)}) collective-permute-start(f32[8,256,256]{2,1,0:T(8,128)S(1)} %get-tuple-element.12), channel_id=1, source_target_pairs={{0,4},{4,0},{1,5},{5,1},{2,6},{6,2},{3,7},{7,3},{8,12},{12,8},{9,1... | collective-permute-start | bytes 6291464 | tf_op jit(solution)/shard_map/ppermute | solution.py:124
  198.1 9.1 %collective-permute-start.6 = (f32[256,256]{1,0:T(8,128)S(1)}, f32[256,256]{1,0:T(8,128)S(1)}, u32[]{:S(2)}, u32[]{:S(2)}) collective-permute-start(f32[256,256]{1,0:T(8,128)S(1)} %slice.9), channel_id=1, source_target_pairs={{0,4},{4,0},{1,5},{5,1},{2,6},{6,2},{3,7},{7,3},{8,12},{12,8},{9,1... | collective-permute-start | bytes 786440 | tf_op jit(solution)/shard_map/ppermute | solution.py:124
  238.8 37.9 %collective-permute-start.8 = (f32[512,256]{1,0:T(8,128)S(1)}, f32[512,256]{1,0:T(8,128)S(1)}, u32[]{:S(2)}, u32[]{:S(2)}) collective-permute-start(f32[512,256]{1,0:T(8,128)S(1)} %pad_maximum_fusion), channel_id=1, source_target_pairs={{0,0},{8,8},{16,1},{24,9},{32,2},{40,10},{48,3},{56,11},{1,16},{9,... | collective-permute-start | bytes 1572872 | tf_op jit(solution)/shard_map/ppermute | solution.py:162
Sparse Core Ops, SparseCore 0:
  136.3 52.5 reduce-scatter.2
  197.2 40.4 reduce-scatter.4

commit v2 on v1

v2 whole, which is shorter than its diff:
```python
import jax
import jax.numpy as jnp
from jax import lax
from jax.experimental import pallas as pl
from jax.experimental.pallas import tpu as pltpu
from jax.sharding import Mesh, PartitionSpec as P

BS = 128
F32 = jnp.float32
BF16 = jnp.bfloat16
VMEM_BYTES = 48 * 1024 * 1024


def cost(flops, bytes_accessed):
    return pl.CostEstimate(flops=flops, bytes_accessed=bytes_accessed, transcendentals=0)


def mask_right_kernel(pattern_ref, values_ref, out_ref):
    at = pl.program_id(0)
    for h in range(4):
        for j in range(2):
            keep = pattern_ref[(2 * at + h // 2) * 2 + j].astype(F32)
            for i in range(2):
                columns = slice(j * BS + i * 64, j * BS + i * 64 + 64)
                top = values_ref[h * 64 : h * 64 + 32, columns]
                bottom = values_ref[h * 64 + 32 : h * 64 + 64, columns]
                out_ref[h, 0, 2 * j + i] = jnp.concatenate([top, bottom], axis=1) * keep


def mask_right(values, pattern):
    return pl.pallas_call(
        mask_right_kernel,
        grid=(4,),
        in_specs=[
            pl.BlockSpec(memory_space=pltpu.SMEM),
            pl.BlockSpec((256, 256), lambda i: (i, 0)),
        ],
        out_specs=pl.BlockSpec((4, 1, 4, 32, 128), lambda i: (0, i, 0, 0, 0)),
        out_shape=jax.ShapeDtypeStruct((4, 4, 4, 32, 128), F32),
        cost_estimate=cost(values.size, 8 * values.size),
    )(pattern.reshape(16), values)


def prepare_kernel(where_ref, b0_ref, b1_ref, b2_ref, b3_ref, high_ref, low_ref):
    xh = where_ref[8]
    for i, ref in enumerate((b0_ref, b1_ref, b2_ref, b3_ref)):
        base = where_ref[4 + i] * 64
        for near in range(2):
            nx = lax.bitwise_xor(xh, jnp.int32(near))
            for pair in range(4):
                even, odd = ref[2 * pair, nx, 0], ref[2 * pair + 1, nx, 0]
                columns = slice(near * 512 + pair * 128, near * 512 + pair * 128 + 128)
                for half in range(2):
                    lanes = slice(half * 64, half * 64 + 64)
                    block = jnp.concatenate([even[:, lanes], odd[:, lanes]], axis=1)
                    high = block.astype(BF16)
                    rows = pl.ds(pl.multiple_of(base + half * 32, 32), 32)
                    high_ref[rows, columns] = high
                    low_ref[rows, columns] = (block - high.astype(F32)).astype(BF16)


def prepare(where, parts):
    spec = pl.BlockSpec((8, 2, 1, 32, 128), lambda t, s: (0, 0, s[t], 0, 0))
    out = pl.BlockSpec((256, 1024), lambda t, s: (t, 0))
    return pl.pallas_call(
        prepare_kernel,
        grid_spec=pltpu.PrefetchScalarGridSpec(
            num_scalar_prefetch=1, grid=(4,), in_specs=[spec] * 4, out_specs=[out] * 2
        ),
        out_shape=[jax.ShapeDtypeStruct((1024, 1024), BF16)] * 2,
        cost_estimate=cost(3 << 20, 8 << 20),
    )(where, *[p.reshape(8, 2, 4, 32, 128) for p in parts])


def product_kernel(half, where_ref, pattern_ref, a0_ref, a1_ref, a2_ref, a3_ref, high_ref, low_ref, out_ref):
    my = pl.program_id(0)
    highs, lows = [], []
    for t, ref in enumerate((a0_ref, a1_ref, a2_ref, a3_ref)):
        rows = []
        for i in range(2):
            row = []
            for j in range(2):
                at = where_ref[t] * 32 + (my * 4 + half * 2 + i) * 2 + j
                row.append(ref[i * BS : (i + 1) * BS, j * BS : (j + 1) * BS] * pattern_ref[at].astype(F32))
            rows.append(jnp.concatenate(row, axis=1))
        block = jnp.concatenate(rows, axis=0)
        high = block.astype(BF16)
        highs.append(high)
        lows.append((block - high.astype(F32)).astype(BF16))
    high = jnp.concatenate(highs, axis=1)
    low = jnp.concatenate(lows, axis=1)
    for near in range(out_ref.shape[1]):
        columns = slice(near * 512, near * 512 + 512)
        terms = jnp.dot(low, high_ref[:, columns], preferred_element_type=F32)
        terms += jnp.dot(high, low_ref[:, columns], preferred_element_type=F32)
        terms += jnp.dot(high, high_ref[:, columns], preferred_element_type=F32)
        for nz in range(8):
            lanes = slice(nz * 64, nz * 64 + 64)
            out_ref[nz, near] = jnp.concatenate([terms[:128, lanes], terms[128:, lanes]], axis=1)


def partial_product(where, pattern, blocks, high, low, half, nears):
    first, count = nears[0], len(nears)
    smem = pl.BlockSpec(memory_space=pltpu.SMEM)
    return pl.pallas_call(
        lambda *refs: product_kernel(half, *refs),
        grid=(4,),
        in_specs=[smem, smem]
        + [pl.BlockSpec((256, 256), lambda i: (2 * i + half, 0))] * 4
        + [pl.BlockSpec((1024, 512 * count), lambda i: (0, first))] * 2,
        out_specs=pl.BlockSpec((8, count, 128, 128), lambda i: (0, 0, i, 0)),
        out_shape=jax.ShapeDtypeStruct((8, count, 512, 128), F32),
        compiler_params=pltpu.CompilerParams(vmem_limit_bytes=VMEM_BYTES),
        cost_estimate=cost((3 << 30) * count, (6 << 20) + (4 << 20) * count),
    )(where, pattern, *blocks, high, low)


def assemble_kernel(first_ref, second_ref, out_ref):
    for half, ref in enumerate((first_ref, second_ref)):
        for lane in range(2):
            rows = slice(half * 256 + lane * 128, half * 256 + lane * 128 + 128)
            lanes = slice(lane * 64, lane * 64 + 64)
            for pair in range(2):
                left, right = ref[2 * pair, :, lanes], ref[2 * pair + 1, :, lanes]
                out_ref[rows, pair * 128 : pair * 128 + 128] = jnp.concatenate([left, right], axis=1)


def assemble(first, second):
    return pl.pallas_call(
        assemble_kernel,
        out_shape=jax.ShapeDtypeStruct((512, 256), F32),
        cost_estimate=cost(0, 1 << 20),
    )(first.reshape(4, 128, 128), second.reshape(4, 128, 128))


def swap(value, axis):
    return lax.ppermute(value, axis, [(0, 1), (1, 0)])


def to_all(value, axis):
    return lax.all_to_all(value, axis, split_axis=0, concat_axis=0, tiled=True)


def body(left_values, left_pattern, right_values, right_pattern):
    xl, core, xh, y = (lax.axis_index(n) for n in ("xl", "core", "xh", "y"))
    turn = 1 - 2 * core
    where = jnp.stack(
        [(y - turn * t + 4) % 4 for t in range(4)]
        + [2 * xl + core, 2 * (1 - xl) + core, 2 * xl + 1 - core, 2 * (1 - xl) + 1 - core, xh]
    ).astype(jnp.int32)

    pattern = lax.all_gather(left_pattern.reshape(32), "y", axis=0, tiled=True)
    ring = [(c * 4 + i, c * 4 + (i + 1 - 2 * c) % 4) for c in range(2) for i in range(4)]
    blocks = [left_values[0]]
    for _ in range(3):
        blocks.append(lax.ppermute(blocks[-1], ("core", "y"), ring))

    right = mask_right(right_values[0], right_pattern[0])
    right = to_all(right.reshape(64, 32, 128), ("xl", "core"))
    right = to_all(right, ("z", "xh", "y"))
    right_far = swap(right, "xl")
    parts = (right, right_far, swap(right, "core"), swap(right_far, "core"))
    high, low = prepare(where, parts)

    send = partial_product(where, pattern, blocks, high, low, 1, (1,))
    both = partial_product(where, pattern, blocks, high, low, 0, (0, 1))
    keep = partial_product(where, pattern, blocks, high, low, 1, (0,))
    got = swap(send, "xh")
    first = lax.psum_scatter(both, "z", scatter_dimension=0, tiled=True)[0]
    second = lax.psum_scatter(keep + got, "z", scatter_dimension=0, tiled=True)[0, 0]
    first = first[0] + swap(first[1], "xh")
    return assemble(to_all(first, "y"), to_all(second, "y"))


def solution(mesh):
    fine = Mesh(mesh.devices.reshape(2, 2, 8, 2, 4), ("xl", "core", "z", "xh", "y"))
    spec = P("y", ("xl", "core"), ("z", "xh"))
    return jax.shard_map(
        body,
        mesh=fine,
        in_specs=(spec,) * 4,
        out_specs=P(("xl", "core", "y"), ("z", "xh")),
        check_vma=False,
    )
```

time: 285 us -> 255 us (0.89)
  waiting for transfers between devices: 169 us -> 116 us
  blocking collectives: 36.7 us -> 58.9 us
    ppermute x1 -> x0, waiting for transfers between devices: 34.1 us -> none  [body(): return lax.ppermute(mine, ('z', 'y'), turned)]
    ppermute x5, waiting for transfers between devices: 80.3 us -> 57.9 us  [swap(): return lax.ppermute(value, axis, [(0, 1), (1, 0)])]
    all_to_all x1 -> x2, waiting for transfers between devices: 25.1 us -> 3.63 us  [to_all(): return lax.all_to_all(value, axis, split_axis=0, concat_axis=0, tiled=True)]
    ppermute x3, waiting for transfers between devices: 0.01 us -> 16.6 us  [body(): blocks.append(lax.ppermute(blocks[-1], ('core', 'y'), ring))]
    all_to_all x2, blocking collectives: 36.7 us -> 51.1 us  [to_all(): return lax.all_to_all(value, axis, split_axis=0, concat_axis=0, tiled=True)]
    reduce_scatter x1, waiting for transfers between devices: 29.5 us -> 38.2 us  [body(): lax.psum_scatter(keep + got, 'z', scatter_dimension=0, tiled=True)[0, 0]]
    unnamed x0 -> x1, blocking collectives: none -> 7.71 us
    ppermute x5, starting transfers between devices: 1.25 us -> 6.14 us  [swap(): return lax.ppermute(value, axis, [(0, 1), (1, 0)])]
  transfers between devices with their start and end apart: 12 -> 12, of which waited for: 7 -> 5; matrix products, arithmetic and copies ran while one was open for 2% -> 3% of each run, Pallas kernels for 7% -> 9%
where the time goes in v2:
time: 255 us; the launch traced here: 252 us
  waiting for transfers between devices  116 us (45%)
  blocking collectives  58.9 us (23%)
  Pallas kernels  36.3 us (14%)
  starting transfers between devices  17.7 us (7%)
  between operations  14.2 us (6%)
  local copies, waits for them, and re-layouts  5.68 us (2%)
    ppermute x5, waiting for transfers between devices, swap(): return lax.ppermute(value, axis, [(0, 1), (1, 0)])  57.9 us
    all_to_all x2, blocking collectives, to_all(): return lax.all_to_all(value, axis, split_axis=0, concat_axis=0, tiled=True)  51.1 us
    reduce_scatter x1, waiting for transfers between devices, body(): lax.psum_scatter(keep + got, 'z', scatter_dimension=0, tiled=True)[0, 0]  38.2 us
    pallas_call x3, Pallas kernels, partial_product(): pl.pallas_call(lambda *refs: product_kernel(half, *refs), grid=(4,), in_s...  24.5 us
    ppermute x3, waiting for transfers between devices, body(): blocks.append(lax.ppermute(blocks[-1], ('core', 'y'), ring))  16.6 us
    all_to_all x2, starting transfers between devices, to_all(): return lax.all_to_all(value, axis, split_axis=0, concat_axis=0, tiled=True)  9.1 us
    unnamed x1, blocking collectives  7.71 us
    ppermute x5, starting transfers between devices, swap(): return lax.ppermute(value, axis, [(0, 1), (1, 0)])  6.14 us
  transfers between devices with their start and end apart: 12, of which 5 were waited for; matrix products, arithmetic and copies ran while one was open for 3% of the time, Pallas kernels for 9%

profile of v2, /device:TPU:56, one launch (start us, length us, event | category | flops | bytes accessed | tf_op | source)
XLA Modules:
  0.0 251.7 jit_solution(9697316973101396416)
XLA Ops:
  6.5 0.2 collective-permute-start
  6.8 0.8 copy.8
  7.5 0.6 reshape_squeeze.3.pattern_ref
  8.1 3.6 %shard_map.46 = f32[4,4,4,32,128]{4,3,2,1,0:T(8,128)} custom-call(s32[16]{0:T(128)} %reshape_squeeze.3.pattern_ref, f32[1024,256]{1,0:T(8,128)} %bitcast.31), custom_call_target="tpu_custom_call" | custom-call | flops 262144 | bytes 2097152 | tf_op jit(solution)/shard_map/pallas_call | solution.py:31
  11.7 0.0 copy-start.6
  11.7 0.0 copy-start.7
  11.7 4.4 %all-to-all-start = ((f32[64,32,128]{2,1,0:T(8,128)}), f32[64,32,128]{2,1,0:T(8,128)}, u32[]{:S(2)}, u32[]{:S(2)}) async-start(f32[64,32,128]{2,1,0:T(8,128)} %bitcast.30), calls=%async_computation | async-start | bytes 2097152 | tf_op jit(solution)/shard_map/all_to_all | solution.py:141
  16.1 0.0 reduce-scatter.3.cloned.1.call-start
  16.2 16.6 %collective-permute-done.refs_3_ = f32[2048,256]{1,0:T(8,128)S(1)} collective-permute-done((f32[2048,256]{1,0:T(8,128)}, f32[2048,256]{1,0:T(8,128)S(1)}, u32[]{:S(2)}, u32[]{:S(2)}) %collective-permute-start) | collective-permute-done | bytes 2097184 | tf_op jit(solution)/shard_map/ppermute | solution.py:156
  32.8 0.0 copy-start.1
  32.8 1.4 collective-permute-start.1
  34.2 0.0 all-to-all-done
  34.2 41.4 %all_to_all.28 = f32[64,32,128]{2,1,0:T(8,128)S(1)} all-to-all(f32[64,32,128]{2,1,0:T(8,128)} %all-to-all-done), channel_id=1, replica_groups=mesh['xl'=2,'core'=2,'z'=8,'xh'=2,'y'=4] {'z','xh','y'}, dimensions={0} | all-to-all | bytes 2097152 | tf_op jit(solution)/shard_map/all_to_all | solution.py:141
  75.6 0.0 copy-start.4
  75.6 0.6 collective-permute-start.3
  76.2 0.0 collective-permute-done.1.refs_4_
  76.2 0.8 collective-permute-start.2
  77.0 0.0 collective-permute-start.4
  77.0 19.7 %collective-permute-done.3 = f32[64,32,128]{2,1,0:T(8,128)} collective-permute-done((f32[64,32,128]{2,1,0:T(8,128)S(1)}, f32[64,32,128]{2,1,0:T(8,128)}, u32[]{:S(2)}, u32[]{:S(2)}) %collective-permute-start.3) | collective-permute-done | bytes 1048608 | tf_op jit(solution)/shard_map/ppermute | solution.py:137
  96.7 0.0 collective-permute-start.5
  96.7 0.0 copy-done.6
  96.7 0.1 copy.7
  96.7 0.1 reshape.37
  96.9 0.0 copy-done.7
  96.9 0.7 dynamic-slice
  98.2 0.2 dynamic-update-slice
  98.5 0.7 stack.39.where_ref.refs_0_
  99.2 7.7 %all-reduce.refs_1_ = s32[128]{0:T(128)S(1)} all-reduce(s32[128]{0:T(128)S(1)} %dynamic-update-slice), channel_id=1, replica_groups=mesh['xl'=2,'core'=2,'z'=8,'xh'=2,'y'=4] {'y'}, use_global_device_ids=true, to_apply=%add | all-reduce | flops 128 | bytes 1024
  106.9 0.0 collective-permute-done.4
  106.9 0.0 collective-permute-done.5
  106.9 0.0 copy-done.1
  106.9 0.0 copy-done.4
  106.9 0.0 copy-start
  106.9 0.0 copy-start.3
  106.9 6.1 %shard_map.47 = (bf16[1024,1024]{1,0:T(8,128)(2,1)}, bf16[1024,1024]{1,0:T(8,128)(2,1)}) custom-call(s32[9]{0:T(128)} %stack.39.where_ref.refs_0_, f32[8,2,4,32,128]{4,3,2,1,0:T(8,128)} %bitcast.29, f32[8,2,4,32,128]{4,3,2,1,0:T(8,128)} %bitcast.14.b1_ref, f32[8,2,4,32,128]{4,3,2,1,0:T(8,128)} %bitcast.15.b2_ref, f32[8,2,4,32,128]{4,3,2,1,0:T(8,128)} %bitcast.16.b3_ref), custom_call_target="tpu_custom_call" | custom-call | flops 3145728 | bytes 8388608 | tf_op jit(solution)/shard_map/pallas_call | solution.py:65
  113.0 0.0 collective-permute-done.2.refs_5_
  113.0 0.0 copy-done
  113.0 0.0 copy-done.3
  113.0 0.0 copy-start.2
  113.0 1.6 copy-done.2
  114.6 11.3 %shard_map.48 = f32[8,2,512,128]{3,2,1,0:T(8,128)} custom-call(s32[9]{0:T(128)S(1)} %copy-done.3, s32[128]{0:T(128)S(1)} %all-reduce.refs_1_, f32[2048,256]{1,0:T(8,128)S(1)} %bitcast.26, f32[2048,256]{1,0:T(8,128)S(1)} %copy-done.2, f32[2048,256]{1,0:T(8,128)} %collective-permute-done.1.refs_4_, f32[2048,256]{1,0:T(8,128)} %collective-permute-done.2.refs_5_, ...), custom_call_target="tpu_custom_call" | custom-call | flops 6442450944 | bytes 14680064 | tf_op jit(solution)/shard_map/pallas_call | solution.py:105
  125.9 0.0 reduce-scatter.3.cloned.1.call-update
  125.9 0.0 reduce-scatter.5.cloned.1.call-start
  126.0 6.6 %shard_map.50 = f32[8,1,512,128]{3,2,1,0:T(8,128)S(1)} custom-call(s32[9]{0:T(128)S(1)} %copy-done.3, s32[128]{0:T(128)S(1)} %all-reduce.refs_1_, f32[2048,256]{1,0:T(8,128)S(1)} %bitcast.27, f32[2048,256]{1,0:T(8,128)} %copy-done.1, f32[2048,256]{1,0:T(8,128)} %collective-permute-done.1.refs_4_, f32[2048,256]{1,0:T(8,128)} %collective-permute-done.2.refs_5_, ...), custom_call_target="tpu_custom_call" | custom-call | flops 3221225472 | bytes 10485760 | tf_op jit(solution)/shard_map/pallas_call | solution.py:105
  132.6 2.8 %collective-permute-start.7 = (f32[8,1,512,128]{3,2,1,0:T(8,128)S(1)}, f32[8,1,512,128]{3,2,1,0:T(8,128)S(1)}, u32[]{:S(2)}, u32[]{:S(2)}) collective-permute-start(f32[8,1,512,128]{3,2,1,0:T(8,128)S(1)} %shard_map.50), channel_id=1, source_target_pairs={{0,4},{4,0},{1,5},{5,1},{2,6},{6,2},{3,7},{7,3},{8,12},{12,8},{9,1... | collective-permute-start | bytes 6291464 | tf_op jit(solution)/shard_map/ppermute | solution.py:137
  135.4 6.7 %shard_map.49 = f32[8,1,512,128]{3,2,1,0:T(8,128)S(1)} custom-call(s32[9]{0:T(128)S(1)} %copy-done.3, s32[128]{0:T(128)S(1)} %all-reduce.refs_1_, f32[2048,256]{1,0:T(8,128)S(1)} %bitcast.28, f32[2048,256]{1,0:T(8,128)} %copy-done.1, f32[2048,256]{1,0:T(8,128)} %collective-permute-done.1.refs_4_, f32[2048,256]{1,0:T(8,128)} %collective-permute-done.2.refs_5_, ...), custom_call_target="tpu_custom_call" | custom-call | flops 3221225472 | bytes 10485760 | tf_op jit(solution)/shard_map/pallas_call | solution.py:105
  142.0 38.2 %collective-permute-done.7 = f32[8,1,512,128]{3,2,1,0:T(8,128)S(1)} collective-permute-done((f32[8,1,512,128]{3,2,1,0:T(8,128)S(1)}, f32[8,1,512,128]{3,2,1,0:T(8,128)S(1)}, u32[]{:S(2)}, u32[]{:S(2)}) %collective-permute-start.7) | collective-permute-done | bytes 2097184 | tf_op jit(solution)/shard_map/ppermute | solution.py:137
  180.2 1.6 add.60
  181.8 0.0 reduce-scatter.5.cloned.1.call-update
  181.8 0.0 reduce-scatter.3.cloned.1.call-done
  181.8 1.0 slice_bitcast_fusion
  182.8 2.8 %collective-permute-start.6 = (f32[512,128]{1,0:T(8,128)S(1)}, f32[512,128]{1,0:T(8,128)S(1)}, u32[]{:S(2)}, u32[]{:S(2)}) collective-permute-start(f32[512,128]{1,0:T(8,128)S(1)} %slice_bitcast_fusion), channel_id=1, source_target_pairs={{0,4},{4,0},{1,5},{5,1},{2,6},{6,2},{3,7},{7,3},{8,12},{12,8},{9,1... | collective-permute-start | bytes 786440 | tf_op jit(solution)/shard_map/ppermute | solution.py:137
  185.6 38.2 %reduce-scatter.5.cloned.1.call-done = f32[1,1,512,128]{3,2,1,0:T(8,128)} async-done(((f32[8,1,512,128]{3,2,1,0:T(8,128)}), f32[1,1,512,128]{3,2,1,0:T(8,128)}) %reduce-scatter.5.cloned.1.call-update) | async-done | bytes 262160 | tf_op jit(solution)/shard_map/reduce_scatter | solution.py:170
  223.8 4.7 %all-to-all-start.3 = ((f32[4,128,128]{2,1,0:T(8,128)}), f32[4,128,128]{2,1,0:T(8,128)S(1)}, u32[]{:S(2)}, u32[]{:S(2)}) async-start(f32[4,128,128]{2,1,0:T(8,128)} %bitcast.33), calls=%async_computation.5 | async-start | bytes 524288 | tf_op jit(solution)/shard_map/all_to_all | solution.py:141
  228.5 0.0 collective-permute-done.6
  228.5 1.0 fusion
  229.5 3.6 %all-to-all-done.3.second_ref = f32[4,128,128]{2,1,0:T(8,128)S(1)} async-done(((f32[4,128,128]{2,1,0:T(8,128)}), f32[4,128,128]{2,1,0:T(8,128)S(1)}, u32[]{:S(2)}, u32[]{:S(2)}) %all-to-all-start.3) | async-done | bytes 262176 | tf_op jit(solution)/shard_map/all_to_all | solution.py:141
  233.1 0.0 copy-start.5
  233.1 9.7 %all_to_all.29.first_ref = f32[4,128,128]{2,1,0:T(8,128)} all-to-all(f32[4,128,128]{2,1,0:T(8,128)S(1)} %bitcast.32), channel_id=1, replica_groups=mesh['xl'=2,'core'=2,'z'=8,'xh'=2,'y'=4] {'y'}, dimensions={0} | all-to-all | bytes 524288 | tf_op jit(solution)/shard_map/all_to_all | solution.py:141
  242.8 0.0 copy-done.5
  242.8 2.0 shard_map.51
  (1 shorter events, 0.0 us)
Async XLA Ops:
  6.5 26.2 %collective-permute-start = (f32[2048,256]{1,0:T(8,128)}, f32[2048,256]{1,0:T(8,128)S(1)}, u32[]{:S(2)}, u32[]{:S(2)}) collective-permute-start(f32[2048,256]{1,0:T(8,128)} %bitcast.25), channel_id=1, source_target_pairs={{0,1},{1,2},{2,3},{3,0},{64,67},{65,64},{66,65},{67,66},{4,5},{5,6... | collective-permute-start | bytes 6291464 | tf_op jit(solution)/shard_map/ppermute | solution.py:156
  11.7 84.9 %copy-start.6 = (s32[1,16,2]{1,2,0:T(2,128)S(1)}, s32[1,16,2]{1,2,0:T(2,128)}, u32[]{:S(2)}) copy-start(s32[1,16,2]{1,2,0:T(2,128)} %param.5) | copy-start | bytes 388
  11.7 85.1 %copy-start.7 = (u32[256]{0:T(256)S(1)}, u32[256]{0:T(256)}, u32[]{:S(2)}) copy-start(u32[256]{0:T(256)} %constant.53) | copy-start | bytes 3076
  11.7 22.5 %all-to-all-start = ((f32[64,32,128]{2,1,0:T(8,128)}), f32[64,32,128]{2,1,0:T(8,128)}, u32[]{:S(2)}, u32[]{:S(2)}) async-start(f32[64,32,128]{2,1,0:T(8,128)} %bitcast.30), calls=%async_computation | async-start | bytes 2097152 | tf_op jit(solution)/shard_map/all_to_all | solution.py:141
  16.1 165.7 %reduce-scatter.3.cloned.1.call-start = ((), (), s32[]{:S(2)}) async-start(), calls=%async_computation.6 | async-start | bytes 4718592 | tf_op jit(solution)/shard_map/reduce_scatter | solution.py:169
  32.8 74.1 %copy-start.1 = (f32[2048,256]{1,0:T(8,128)}, f32[2048,256]{1,0:T(8,128)S(1)}, u32[]{:S(2)}) copy-start(f32[2048,256]{1,0:T(8,128)S(1)} %collective-permute-done.refs_3_) | copy-start | bytes 6291460
  32.8 43.4 %collective-permute-start.1 = (f32[2048,256]{1,0:T(8,128)S(1)}, f32[2048,256]{1,0:T(8,128)}, u32[]{:S(2)}, u32[]{:S(2)}) collective-permute-start(f32[2048,256]{1,0:T(8,128)S(1)} %collective-permute-done.refs_3_), channel_id=1, source_target_pairs={{0,1},{1,2},{2,3},{3,0},{64,67},{65,64},{66,65},{67,66},{4,5},{5,6... | collective-permute-start | bytes 6291464 | tf_op jit(solution)/shard_map/ppermute | solution.py:156
  75.6 31.3 %copy-start.4 = (f32[64,32,128]{2,1,0:T(8,128)}, f32[64,32,128]{2,1,0:T(8,128)S(1)}, u32[]{:S(2)}) copy-start(f32[64,32,128]{2,1,0:T(8,128)S(1)} %all_to_all.28) | copy-start | bytes 3145732
  75.6 21.0 %collective-permute-start.3 = (f32[64,32,128]{2,1,0:T(8,128)S(1)}, f32[64,32,128]{2,1,0:T(8,128)}, u32[]{:S(2)}, u32[]{:S(2)}) collective-permute-start(f32[64,32,128]{2,1,0:T(8,128)S(1)} %all_to_all.28), channel_id=1, source_target_pairs={{0,128},{128,0},{1,129},{129,1},{2,130},{130,2},{3,131},{131,3},{4... | collective-permute-start | bytes 3145736 | tf_op jit(solution)/shard_map/ppermute | solution.py:137
  76.2 36.8 %collective-permute-start.2 = (f32[2048,256]{1,0:T(8,128)}, f32[2048,256]{1,0:T(8,128)}, u32[]{:S(2)}, u32[]{:S(2)}) collective-permute-start(f32[2048,256]{1,0:T(8,128)} %collective-permute-done.1.refs_4_), channel_id=1, source_target_pairs={{0,1},{1,2},{2,3},{3,0},{64,67},{65,64},{66,65},{67,66},{4,5},{5,6... | collective-permute-start | bytes 6291464 | tf_op jit(solution)/shard_map/ppermute | solution.py:156
  77.0 29.9 %collective-permute-start.4 = (f32[64,32,128]{2,1,0:T(8,128)S(1)}, f32[64,32,128]{2,1,0:T(8,128)}, u32[]{:S(2)}, u32[]{:S(2)}) collective-permute-start(f32[64,32,128]{2,1,0:T(8,128)S(1)} %all_to_all.28), channel_id=1, source_target_pairs={{0,64},{64,0},{1,65},{65,1},{2,66},{66,2},{3,67},{67,3},{4,68},{68... | collective-permute-start | bytes 3145736 | tf_op jit(solution)/shard_map/ppermute | solution.py:137
  96.7 10.2 %collective-permute-start.5 = (f32[64,32,128]{2,1,0:T(8,128)}, f32[64,32,128]{2,1,0:T(8,128)}, u32[]{:S(2)}, u32[]{:S(2)}) collective-permute-start(f32[64,32,128]{2,1,0:T(8,128)} %collective-permute-done.3), channel_id=1, source_target_pairs={{0,64},{64,0},{1,65},{65,1},{2,66},{66,2},{3,67},{67,3},{4,68},{68... | collective-permute-start | bytes 3145736 | tf_op jit(solution)/shard_map/ppermute | solution.py:137
  106.9 6.1 %copy-start = (f32[1,2048,256]{2,1,0:T(8,128)S(1)}, f32[1,2048,256]{2,1,0:T(8,128)}, u32[]{:S(2)}) copy-start(f32[1,2048,256]{2,1,0:T(8,128)} %param.4) | copy-start | bytes 6291460
  106.9 6.1 %copy-start.3 = (s32[9]{0:T(128)S(1)}, s32[9]{0:T(128)}, u32[]{:S(2)}) copy-start(s32[9]{0:T(128)} %stack.39.where_ref.refs_0_) | copy-start | bytes 112
  113.0 1.6 copy-start.2
  125.9 97.9 %reduce-scatter.5.cloned.1.call-start = ((), (), s32[]{:S(2)}) async-start(), calls=%async_computation.7 | async-start | bytes 2359296 | tf_op jit(solution)/shard_map/reduce_scatter | solution.py:170
  132.6 47.6 %collective-permute-start.7 = (f32[8,1,512,128]{3,2,1,0:T(8,128)S(1)}, f32[8,1,512,128]{3,2,1,0:T(8,128)S(1)}, u32[]{:S(2)}, u32[]{:S(2)}) collective-permute-start(f32[8,1,512,128]{3,2,1,0:T(8,128)S(1)} %shard_map.50), channel_id=1, source_target_pairs={{0,4},{4,0},{1,5},{5,1},{2,6},{6,2},{3,7},{7,3},{8,12},{12,8},{9,1... | collective-permute-start | bytes 6291464 | tf_op jit(solution)/shard_map/ppermute | solution.py:137
  182.8 45.7 %collective-permute-start.6 = (f32[512,128]{1,0:T(8,128)S(1)}, f32[512,128]{1,0:T(8,128)S(1)}, u32[]{:S(2)}, u32[]{:S(2)}) collective-permute-start(f32[512,128]{1,0:T(8,128)S(1)} %slice_bitcast_fusion), channel_id=1, source_target_pairs={{0,4},{4,0},{1,5},{5,1},{2,6},{6,2},{3,7},{7,3},{8,12},{12,8},{9,1... | collective-permute-start | bytes 786440 | tf_op jit(solution)/shard_map/ppermute | solution.py:137
  223.8 9.3 %all-to-all-start.3 = ((f32[4,128,128]{2,1,0:T(8,128)}), f32[4,128,128]{2,1,0:T(8,128)S(1)}, u32[]{:S(2)}, u32[]{:S(2)}) async-start(f32[4,128,128]{2,1,0:T(8,128)} %bitcast.33), calls=%async_computation.5 | async-start | bytes 524288 | tf_op jit(solution)/shard_map/all_to_all | solution.py:141
  233.1 9.7 %copy-start.5 = (f32[4,128,128]{2,1,0:T(8,128)}, f32[4,128,128]{2,1,0:T(8,128)S(1)}, u32[]{:S(2)}) copy-start(f32[4,128,128]{2,1,0:T(8,128)S(1)} %all-to-all-done.3.second_ref) | copy-start | bytes 786436
Sparse Core Ops, SparseCore 0:
  126.0 53.2 reduce-scatter.2
  181.9 41.8 reduce-scatter.4

commit v3 on v0

v3 whole, which is shorter than its diff:
```python
import jax
import jax.numpy as jnp
from jax import lax
from jax.experimental import pallas as pl
from jax.experimental.pallas import tpu as pltpu
from jax.sharding import Mesh, PartitionSpec as P

BS = 128
F32 = jnp.float32
BF16 = jnp.bfloat16
VMEM_BYTES = 56 * 1024 * 1024


LIGHT = pl.CostEstimate(flops=1, bytes_accessed=1, transcendentals=0)


def mask_right_kernel(pattern_ref, values_ref, out_ref):
    at = pl.program_id(0)
    for h in range(4):
        for j in range(2):
            keep = pattern_ref[(2 * at + h // 2) * 2 + j].astype(F32)
            for i in range(2):
                columns = slice(j * BS + i * 64, j * BS + i * 64 + 64)
                top = values_ref[h * 64 : h * 64 + 32, columns]
                bottom = values_ref[h * 64 + 32 : h * 64 + 64, columns]
                out_ref[h, 0, 2 * j + i] = jnp.concatenate([top, bottom], axis=1) * keep


def mask_right(values, pattern):
    return pl.pallas_call(
        mask_right_kernel,
        grid=(4,),
        in_specs=[
            pl.BlockSpec(memory_space=pltpu.SMEM),
            pl.BlockSpec((256, 256), lambda i: (i, 0)),
        ],
        out_specs=pl.BlockSpec((4, 1, 4, 32, 128), lambda i: (0, i, 0, 0, 0)),
        out_shape=jax.ShapeDtypeStruct((4, 4, 4, 32, 128), F32),
        cost_estimate=LIGHT,
    )(pattern.reshape(16), values)


def split(block):
    high = block.astype(BF16)
    return high, (block - high.astype(F32)).astype(BF16)


def prepare_kernel(where_ref, b0_ref, b1_ref, high_ref, low_ref):
    core, xh, z = where_ref[4], where_ref[6], where_ref[7]
    for i, ref in enumerate((b0_ref, b1_ref)):
        base = lax.bitwise_xor(core, jnp.int32(i)) * 64
        for near in range(2):
            nx = lax.bitwise_xor(xh, jnp.int32(near))
            for pair in range(4):
                even = ref[lax.bitwise_and(z + 2 * pair, 7), nx, 0]
                odd = ref[lax.bitwise_and(z + 2 * pair + 1, 7), nx, 0]
                columns = slice(pair * 256 + near * 128, pair * 256 + near * 128 + 128)
                for half in range(2):
                    lanes = slice(half * 64, half * 64 + 64)
                    high, low = split(jnp.concatenate([even[:, lanes], odd[:, lanes]], axis=1))
                    rows = pl.ds(pl.multiple_of(base + half * 32, 32), 32)
                    high_ref[rows, columns] = high
                    low_ref[rows, columns] = low


def prepare(where, mine, other):
    spec = pl.BlockSpec((8, 2, 1, 32, 128), lambda t, s: (0, 0, s[t], 0, 0))
    out = pl.BlockSpec((128, 1024), lambda t, s: (t, 0))
    return pl.pallas_call(
        prepare_kernel,
        grid_spec=pltpu.PrefetchScalarGridSpec(
            num_scalar_prefetch=1, grid=(4,), in_specs=[spec] * 2, out_specs=[out] * 2
        ),
        out_shape=[jax.ShapeDtypeStruct((512, 1024), BF16)] * 2,
        cost_estimate=LIGHT,
    )(where, mine.reshape(8, 2, 4, 32, 128), other.reshape(8, 2, 4, 32, 128))


def split_kernel(block_ref, high_ref, low_ref):
    high_ref[...], low_ref[...] = split(block_ref[...])


def split_block(block):
    spec = pl.BlockSpec((2, 512, 256), lambda i: (i, 0, 0))
    return pl.pallas_call(
        split_kernel,
        grid=(2,),
        in_specs=[spec],
        out_specs=[spec] * 2,
        out_shape=[jax.ShapeDtypeStruct((4, 512, 256), BF16)] * 2,
        cost_estimate=LIGHT,
    )(block.reshape(4, 512, 256))


def product_kernel(count, where_ref, *refs):
    weights, blocks, out_ref = refs[: 4 * count], refs[4 * count : -1], refs[-1]
    sides = []
    for far in range(2):
        lanes = pl.ds(pl.multiple_of(lax.bitwise_xor(where_ref[5], jnp.int32(far)) * BS, BS), BS)
        sides.append([jnp.concatenate([ref[0, :, lanes] for ref in blocks[i::2]], axis=1) for i in range(2)])
    for at in range(count):
        terms = jnp.zeros((512, 256), F32)
        for far, (high, low) in enumerate(sides):
            w_high, w_low = (ref[...] for ref in weights[4 * at + 2 * far : 4 * at + 2 * far + 2])
            terms += jnp.dot(low, w_high, preferred_element_type=F32)
            terms += jnp.dot(high, w_low, preferred_element_type=F32)
            terms += jnp.dot(high, w_high, preferred_element_type=F32)
        for near in range(2):
            for odd in range(2):
                lanes = slice(near * 128 + odd * 64, near * 128 + odd * 64 + 64)
                out_ref[2 * at + odd, near, 0] = jnp.concatenate([terms[:256, lanes], terms[256:, lanes]], axis=1)


def partial_product(where, weights, blocks, pairs):
    n = 2 * len(pairs)
    block = pl.BlockSpec((1, 512, 256), lambda i, s: (lax.bitwise_and(s[8] + i, 3), 0, 0))
    columns = []
    for pair in pairs:
        columns += [pl.BlockSpec((512, 256), lambda i, s, pair=pair: (0, pair))] * 4
    return pl.pallas_call(
        lambda *refs: product_kernel(len(pairs), *refs),
        grid_spec=pltpu.PrefetchScalarGridSpec(
            num_scalar_prefetch=1,
            grid=(4,),
            in_specs=columns + [block] * 8,
            out_specs=pl.BlockSpec((n, 2, 1, 256, 128), lambda i, s: (0, 0, i, 0, 0)),
        ),
        out_shape=jax.ShapeDtypeStruct((n, 2, 4, 256, 128), F32),
        compiler_params=pltpu.CompilerParams(vmem_limit_bytes=VMEM_BYTES),
        cost_estimate=LIGHT,
    )(where, *(weights * len(pairs)), *blocks)


def assemble_kernel(where_ref, p0_ref, p1_ref, p2_ref, p3_ref, out_ref, held):
    for t, ref in enumerate((p0_ref, p1_ref, p2_ref, p3_ref)):
        held[lax.bitwise_and(where_ref[8] + 4 - t, 3)] = ref[...]
    for half in range(2):
        lanes = slice(half * 64, half * 64 + 64)
        for pair in range(2):
            both = jnp.concatenate([held[2 * pair, :, lanes], held[2 * pair + 1, :, lanes]], axis=1)
            out_ref[half * 256 : half * 256 + 256, pair * 128 : pair * 128 + 128] = both


def assemble(where, pieces):
    return pl.pallas_call(
        assemble_kernel,
        in_specs=[pl.BlockSpec(memory_space=pltpu.SMEM)] + [pl.BlockSpec(memory_space=pltpu.VMEM)] * 4,
        out_specs=pl.BlockSpec(memory_space=pltpu.VMEM),
        out_shape=jax.ShapeDtypeStruct((512, 256), F32),
        scratch_shapes=[pltpu.VMEM((4, 256, 128), F32)],
        cost_estimate=LIGHT,
    )(where, *pieces)


def swap(value, axis):
    return lax.ppermute(value, axis, [(0, 1), (1, 0)])


def to_all(value, axis):
    return lax.all_to_all(value, axis, split_axis=0, concat_axis=0, tiled=True)


def shift(value, axis, size, step):
    return lax.ppermute(value, axis, [(i, (i + step) % size) for i in range(size)])


def tie(*values):
    return lax.optimization_barrier(values)


def send_both(right, left):
    return shift(right, "z", 8, 1), shift(left, "z", 8, -1)


def sum_over_z(ahead, behind):
    def first(own):
        return send_both(own(4)[:2], own(4)[2:])

    def second(own, right, left):
        return send_both(
            jnp.concatenate([own(3)[:2] + right, own(3)[2:]]), jnp.concatenate([own(5)[:2], own(5)[2:] + left])
        )

    def later(own, k, right, left):
        return send_both(own(k) + right, own(8 - k) + left)

    a = first(ahead)
    b = first(behind)
    a = second(ahead, *a)
    b = second(behind, *b)
    a = later(ahead, 2, *a)
    a, b = tie(a, b)
    a = later(ahead, 1, *a)
    b = later(behind, 2, *b)
    a, b = tie(a, b)
    away = swap(ahead(0) + a[0] + a[1], "xh")
    b = later(behind, 1, *b)
    return behind(0) + b[0] + b[1] + away


def body(left_values, left_pattern, right_values, right_pattern):
    xl, core, xh, y, z = (lax.axis_index(n) for n in ("xl", "core", "xh", "y", "z"))
    turn = 1 - 2 * core
    where = jnp.stack([(y - turn * t + 4) % 4 for t in range(4)] + [core, xl, xh, z, y]).astype(jnp.int32)
    ring = [(c * 4 + i, c * 4 + (i + 1 - 2 * c) % 4) for c in range(2) for i in range(4)]

    keep = jnp.repeat(left_pattern[0].astype(F32), BS, axis=1)
    left = (left_values[0].reshape(16, BS, 256) * keep[:, None, :]).reshape(2048, 256)
    left, right_values, where = tie(left, right_values, where)
    left1 = lax.ppermute(left, ("core", "y"), ring)

    right = mask_right(right_values[0], right_pattern[0])
    right = to_all(right.reshape(64, 32, 128), ("xl", "core"))
    left1, right = tie(left1, right)
    left2 = lax.ppermute(left1, ("core", "y"), ring)
    right = to_all(right, ("z", "xh", "y"))
    left2, right = tie(left2, right)
    left3 = lax.ppermute(left2, ("core", "y"), ring)
    blocks = (left, left1, left2, left3)
    right_far = swap(right, "xl")
    weights = prepare(where, right, swap(right, "core"))
    halves = [half for block in blocks[:3] for half in split_block(block)]
    right_far, weights, halves = tie(right_far, weights, halves)
    halves += split_block(blocks[3])
    weights = (*weights, *prepare(where, right_far, swap(right_far, "core")))

    middle = partial_product(where, weights, halves, (2,))
    weights, middle = tie(weights, middle)
    third = partial_product(where, weights, halves, (1,))
    weights, third = tie(weights, third)
    others = partial_product(where, weights, halves, (0, 3))
    chunks = [others[0], others[1], third[0], third[1], middle[0], middle[1], others[2], others[3]]
    mine = sum_over_z(lambda k: chunks[k][1], lambda k: chunks[k][0])
    pieces = [mine[0]] + [shift(mine[t], "y", 4, t) for t in (1, 2, 3)]
    return assemble(where, pieces)


def solution(mesh):
    fine = Mesh(mesh.devices.reshape(2, 2, 8, 2, 4), ("xl", "core", "z", "xh", "y"))
    spec = P("y", ("xl", "core"), ("z", "xh"))
    return jax.shard_map(
        body,
        mesh=fine,
        in_specs=(spec,) * 4,
        out_specs=P(("xl", "core", "y"), ("z", "xh")),
        check_vma=False,
    )
```

time: 781 us -> 231 us (0.30)
  waiting for transfers between devices: 704 us -> 71.4 us
  blocking collectives: 0 us -> 59.1 us
  Pallas kernels: 0 us -> 56.1 us
  matrix products: 32.7 us -> 0 us
  starting transfers between devices: 9.83 us -> 27.2 us
  between operations: 13.2 us -> 0.27 us
  local copies, waits for them, and re-layouts: 15.3 us -> 6.53 us
    reduce_scatter x2 -> x0, waiting for transfers between devices: 565 us -> none  [the longest x1 533 us: body(): lax.psum_scatter(terms, 'col', scatter_dimension=1, tiled=True)]
    all_to_all x1 -> x0, waiting for transfers between devices: 87.9 us -> none  [body(): lax.all_to_all(right_slab, 'col', split_axis=0, concat_axis=1, tiled=True)]
    ppermute x0 -> x26, waiting for transfers between devices: none -> 71.4 us  [the longest x19 53.1 us: shift(): lax.ppermute(value, axis, [(i, (i + step) % size) for i in range(size)])]
    all_to_all x0 -> x2, blocking collectives: none -> 59.1 us  [to_all(): return lax.all_to_all(value, axis, split_axis=0, concat_axis=0, tiled=True)]
    pallas_call x0 -> x11, Pallas kernels: none -> 56.1 us  [the longest x3 29.9 us: partial_product(): pl.pallas_call(lambda *refs: product_kernel(len(pairs), *refs), grid_spec...]
    all_gather x1 -> x0, waiting for transfers between devices: 51 us -> none  [body(): right_slab = lax.all_gather(right, 'row', axis=0, tiled=True)]
    dot_general x1 -> x0, matrix products: 32.7 us -> none  [body(): jnp.dot(left, right_panel, preferred_element_type=jnp.float32, precision=...]
    ppermute x0 -> x26, starting transfers between devices: none -> 27.2 us  [the longest x19 21.6 us: shift(): lax.ppermute(value, axis, [(i, (i + step) % size) for i in range(size)])]
  transfers between devices with their start and end apart: 4 -> 26, of which waited for: 4 -> 14; matrix products, arithmetic and copies ran while one was open for 1% -> 2% of each run, Pallas kernels for 0% -> 18%
where the time goes in v3:
time: 231 us; the launch traced here: 227 us
  waiting for transfers between devices  71.4 us (31%)
  blocking collectives  59.1 us (26%)
  Pallas kernels  56.1 us (24%)
  starting transfers between devices  27.2 us (12%)
  other arithmetic  6.63 us (3%)
  local copies, waits for them, and re-layouts  6.53 us (3%)
    all_to_all x2, blocking collectives, to_all(): return lax.all_to_all(value, axis, split_axis=0, concat_axis=0, tiled=True)  59.1 us
    ppermute x19, waiting for transfers between devices, shift(): lax.ppermute(value, axis, [(i, (i + step) % size) for i in range(size)])  53.1 us
    pallas_call x3, Pallas kernels, partial_product(): pl.pallas_call(lambda *refs: product_kernel(len(pairs), *refs), grid_spec...  29.9 us
    ppermute x19, starting transfers between devices, shift(): lax.ppermute(value, axis, [(i, (i + step) % size) for i in range(size)])  21.6 us
    ppermute x4, waiting for transfers between devices, swap(): return lax.ppermute(value, axis, [(0, 1), (1, 0)])  13.5 us
    pallas_call x4, Pallas kernels, split_block(): pl.pallas_call(split_kernel, grid=(2,), in_specs=[spec], out_specs=[spec]...  10.6 us
    pallas_call x2, Pallas kernels, prepare(): pl.pallas_call(prepare_kernel, grid_spec=pltpu.PrefetchScalarGridSpec(num...  9.71 us
  transfers between devices with their start and end apart: 26, of which 14 were waited for; matrix products, arithmetic and copies ran while one was open for 2% of the time, Pallas kernels for 18%

profile of v3, /device:TPU:56, one launch (start us, length us, event | category | flops | bytes accessed | tf_op | source)
XLA Modules:
  0.0 227.2 jit_solution(10755363860506271796)
XLA Ops:
  0.0 0.7 convert_bitcast_fusion
  0.9 1.7 bitcast_multiply_fusion
  2.7 0.8 stack.39.where_ref.refs_0_
  3.5 0.2 collective-permute-start
  3.8 0.6 reshape_squeeze.7.pattern_ref
  4.4 3.6 %shard_map.46 = f32[4,4,4,32,128]{4,3,2,1,0:T(8,128)} custom-call(s32[16]{0:T(128)} %reshape_squeeze.7.pattern_ref, f32[1024,256]{1,0:T(8,128)} %bitcast.107), custom_call_target="tpu_custom_call" | custom-call | flops 1 | bytes 1 | tf_op jit(solution)/shard_map/pallas_call | solution.py:30
  8.0 17.9 %all_to_all.10 = f32[64,32,128]{2,1,0:T(8,128)S(1)} all-to-all(f32[64,32,128]{2,1,0:T(8,128)} %bitcast.105), channel_id=1, replica_groups=mesh['xl'=2,'core'=2,'z'=8,'xh'=2,'y'=4] {'xl','core'}, dimensions={0} | all-to-all | bytes 2097152 | tf_op jit(solution)/shard_map/all_to_all | solution.py:160
  25.9 3.7 %collective-permute-done = f32[2048,256]{1,0:T(8,128)} collective-permute-done((f32[2048,256]{1,0:T(8,128)S(1)}, f32[2048,256]{1,0:T(8,128)}, u32[]{:S(2)}, u32[]{:S(2)}) %collective-permute-start) | collective-permute-done | bytes 2097184 | tf_op jit(solution)/shard_map/ppermute | solution.py:210
  29.6 1.4 collective-permute-start.1
  31.0 41.2 %all_to_all.11 = f32[64,32,128]{2,1,0:T(8,128)S(1)} all-to-all(f32[64,32,128]{2,1,0:T(8,128)S(1)} %all_to_all.10), channel_id=1, replica_groups=mesh['xl'=2,'core'=2,'z'=8,'xh'=2,'y'=4] {'z','xh','y'}, dimensions={0} | all-to-all | bytes 2097152 | tf_op jit(solution)/shard_map/all_to_all | solution.py:160
  72.2 0.1 collective-permute-start.3
  72.3 0.7 collective-permute-start.2
  73.0 0.8 collective-permute-start.5
  73.7 2.6 %shard_map.48 = (bf16[4,512,256]{2,1,0:T(8,128)(2,1)}, bf16[4,512,256]{2,1,0:T(8,128)(2,1)}) custom-call(f32[4,512,256]{2,1,0:T(8,128)} %bitcast.103), custom_call_target="tpu_custom_call" | custom-call | flops 1 | bytes 1 | tf_op jit(solution)/shard_map/pallas_call | solution.py:85
  76.4 2.7 %shard_map.49 = (bf16[4,512,256]{2,1,0:T(8,128)(2,1)}, bf16[4,512,256]{2,1,0:T(8,128)(2,1)}) custom-call(f32[4,512,256]{2,1,0:T(8,128)} %bitcast.17.block_ref), custom_call_target="tpu_custom_call" | custom-call | flops 1 | bytes 1 | tf_op jit(solution)/shard_map/pallas_call | solution.py:85
  79.1 2.6 %shard_map.50 = (bf16[4,512,256]{2,1,0:T(8,128)(2,1)}, bf16[4,512,256]{2,1,0:T(8,128)(2,1)}) custom-call(f32[4,512,256]{2,1,0:T(8,128)} %bitcast.106), custom_call_target="tpu_custom_call" | custom-call | flops 1 | bytes 1 | tf_op jit(solution)/shard_map/pallas_call | solution.py:85
  81.7 4.9 %shard_map.47 = (bf16[512,1024]{1,0:T(8,128)(2,1)}, bf16[512,1024]{1,0:T(8,128)(2,1)}) custom-call(s32[9]{0:T(128)} %stack.39.where_ref.refs_0_, f32[8,2,4,32,128]{4,3,2,1,0:T(8,128)} %bitcast.104, f32[8,2,4,32,128]{4,3,2,1,0:T(8,128)} %bitcast.15.b1_ref), custom_call_target="tpu_custom_call" | custom-call | flops 1 | bytes 1 | tf_op jit(solution)/shard_map/pallas_call | solution.py:69
  86.6 11.4 %collective-permute-done.2 = f32[64,32,128]{2,1,0:T(8,128)} collective-permute-done((f32[64,32,128]{2,1,0:T(8,128)S(1)}, f32[64,32,128]{2,1,0:T(8,128)}, u32[]{:S(2)}, u32[]{:S(2)}) %collective-permute-start.2) | collective-permute-done | bytes 1048608 | tf_op jit(solution)/shard_map/ppermute | solution.py:156
  98.0 1.1 collective-permute-done.5
  99.1 2.6 %shard_map.52 = (bf16[4,512,256]{2,1,0:T(8,128)(2,1)}, bf16[4,512,256]{2,1,0:T(8,128)(2,1)}) custom-call(f32[4,512,256]{2,1,0:T(8,128)} %bitcast.21.block_ref), custom_call_target="tpu_custom_call" | custom-call | flops 1 | bytes 1 | tf_op jit(solution)/shard_map/pallas_call | solution.py:85
  101.8 1.0 copy-done.5
  102.8 4.8 %shard_map.51 = (bf16[512,1024]{1,0:T(8,128)(2,1)}, bf16[512,1024]{1,0:T(8,128)(2,1)}) custom-call(s32[9]{0:T(128)} %stack.39.where_ref.refs_0_, f32[8,2,4,32,128]{4,3,2,1,0:T(8,128)} %bitcast.19.b0_ref, f32[8,2,4,32,128]{4,3,2,1,0:T(8,128)} %bitcast.108), custom_call_target="tpu_custom_call" | custom-call | flops 1 | bytes 1 | tf_op jit(solution)/shard_map/pallas_call | solution.py:69
  107.6 8.7 %shard_map.53 = f32[2,2,4,256,128]{4,3,2,1,0:T(8,128)} custom-call(s32[9]{0:T(128)} %stack.39.where_ref.refs_0_, bf16[512,1024]{1,0:T(8,128)(2,1)} %get-tuple-element.83.refs_1_.refs_5_, bf16[512,1024]{1,0:T(8,128)(2,1)} %get-tuple-element.84.refs_2_.refs_6_, bf16[512,1024]{1,0:T(8,128)(2,1)} %get-tuple-element.85.refs_3_.refs_7_, ...), custom_call_target="tpu_custom_call" | custom-call | flops 1 | bytes 1 | tf_op jit(solution)/shard_map/pallas_call | solution.py:120
  116.3 1.4 slice_bitcast_fusion.9
  117.8 1.0 collective-permute-start.12
  118.7 0.8 collective-permute-start.6
  119.5 1.2 collective-permute-start.14
  120.7 2.4 %collective-permute-start.9 = (f32[2,256,128]{2,1,0:T(8,128)S(1)}, f32[2,256,128]{2,1,0:T(8,128)S(1)}, u32[]{:S(2)}, u32[]{:S(2)}) collective-permute-start(f32[2,256,128]{2,1,0:T(8,128)S(1)} %get-tuple-element.106), channel_id=1, source_target_pairs={{0,56},{8,0},{16,8},{24,16},{32,24},{40,32},{48,40},{56,48},{1,57}... | collective-permute-start | bytes 786440 | tf_op jit(solution)/shard_map/ppermute | solution.py:164
  123.1 8.7 %shard_map.54 = f32[2,2,4,256,128]{4,3,2,1,0:T(8,128)} custom-call(s32[9]{0:T(128)} %stack.39.where_ref.refs_0_, bf16[512,1024]{1,0:T(8,128)(2,1)} %get-tuple-element.83.refs_1_.refs_5_, bf16[512,1024]{1,0:T(8,128)(2,1)} %get-tuple-element.84.refs_2_.refs_6_, bf16[512,1024]{1,0:T(8,128)(2,1)} %get-tuple-element.85.refs_3_.refs_7_, ...), custom_call_target="tpu_custom_call" | custom-call | flops 1 | bytes 1 | tf_op jit(solution)/shard_map/pallas_call | solution.py:120
  131.8 1.1 slice_bitcast_fusion.10
  132.9 1.1 bitcast_add_fusion.3
  134.1 0.3 collective-permute-start.7
  134.3 1.1 bitcast_add_fusion.2
  135.5 2.1 collective-permute-start.10
  137.6 12.5 %shard_map.55 = f32[4,2,4,256,128]{4,3,2,1,0:T(8,128)} custom-call(s32[9]{0:T(128)} %stack.39.where_ref.refs_0_, bf16[512,1024]{1,0:T(8,128)(2,1)} %get-tuple-element.83.refs_1_.refs_5_, bf16[512,1024]{1,0:T(8,128)(2,1)} %get-tuple-element.84.refs_2_.refs_6_, bf16[512,1024]{1,0:T(8,128)(2,1)} %get-tuple-element.85.refs_3_.refs_7_, ...), custom_call_target="tpu_custom_call" | custom-call | flops 1 | bytes 1 | tf_op jit(solution)/shard_map/pallas_call | solution.py:120
  150.1 2.4 %collective-permute-start.15 = (f32[4,256,128]{2,1,0:T(8,128)S(1)}, f32[4,256,128]{2,1,0:T(8,128)S(1)}, u32[]{:S(2)}, u32[]{:S(2)}) collective-permute-start(f32[4,256,128]{2,1,0:T(8,128)S(1)} %pad_maximum_fusion.3), channel_id=1, source_target_pairs={{0,56},{8,0},{16,8},{24,16},{32,24},{40,32},{48,40},{56,48},{1,57}... | collective-permute-start | bytes 1572872 | tf_op jit(solution)/shard_map/ppermute | solution.py:164
  152.9 1.2 fusion.5
  154.1 1.9 collective-permute-start.11
  156.1 9.0 %collective-permute-done.15 = f32[4,256,128]{2,1,0:T(8,128)S(1)} collective-permute-done((f32[4,256,128]{2,1,0:T(8,128)S(1)}, f32[4,256,128]{2,1,0:T(8,128)S(1)}, u32[]{:S(2)}, u32[]{:S(2)}) %collective-permute-start.15) | collective-permute-done | bytes 524320 | tf_op jit(solution)/shard_map/ppermute | solution.py:164
  165.1 2.4 %collective-permute-done.13 = f32[4,256,128]{2,1,0:T(8,128)S(1)} collective-permute-done((f32[4,256,128]{2,1,0:T(8,128)S(1)}, f32[4,256,128]{2,1,0:T(8,128)S(1)}, u32[]{:S(2)}, u32[]{:S(2)}) %collective-permute-start.13) | collective-permute-done | bytes 524320 | tf_op jit(solution)/shard_map/ppermute | solution.py:164
  167.5 8.8 %collective-permute-done.8 = f32[4,256,128]{2,1,0:T(8,128)S(1)} collective-permute-done((f32[4,256,128]{2,1,0:T(8,128)S(1)}, f32[4,256,128]{2,1,0:T(8,128)S(1)}, u32[]{:S(2)}, u32[]{:S(2)}) %collective-permute-start.8) | collective-permute-done | bytes 524320 | tf_op jit(solution)/shard_map/ppermute | solution.py:164
  176.4 0.2 fusion.3
  176.6 1.6 collective-permute-start.19
  178.2 0.1 collective-permute-start.17
  178.3 1.9 collective-permute-start.16
  180.2 0.5 collective-permute-start.18
  180.7 10.8 %collective-permute-done.19 = f32[4,256,128]{2,1,0:T(8,128)S(1)} collective-permute-done((f32[4,256,128]{2,1,0:T(8,128)S(1)}, f32[4,256,128]{2,1,0:T(8,128)S(1)}, u32[]{:S(2)}, u32[]{:S(2)}) %collective-permute-start.19) | collective-permute-done | bytes 524320 | tf_op jit(solution)/shard_map/ppermute | solution.py:164
  191.5 7.8 %collective-permute-done.17 = f32[4,256,128]{2,1,0:T(8,128)S(1)} collective-permute-done((f32[4,256,128]{2,1,0:T(8,128)S(1)}, f32[4,256,128]{2,1,0:T(8,128)S(1)}, u32[]{:S(2)}, u32[]{:S(2)}) %collective-permute-start.17) | collective-permute-done | bytes 524320 | tf_op jit(solution)/shard_map/ppermute | solution.py:164
  199.3 2.0 collective-permute-done.18
  201.4 0.2 fusion.7
  201.6 2.0 collective-permute-start.20
  203.5 2.4 %collective-permute-start.22 = (f32[4,256,128]{2,1,0:T(8,128)S(1)}, f32[4,256,128]{2,1,0:T(8,128)S(1)}, u32[]{:S(2)}, u32[]{:S(2)}) collective-permute-start(f32[4,256,128]{2,1,0:T(8,128)S(1)} %get-tuple-element.98), channel_id=1, source_target_pairs={{0,4},{4,0},{1,5},{5,1},{2,6},{6,2},{3,7},{7,3},{8,12},{12,8},{9,1... | collective-permute-start | bytes 1572872 | tf_op jit(solution)/shard_map/ppermute | solution.py:156
  205.9 0.1 collective-permute-start.21
  206.0 6.2 %collective-permute-done.20 = f32[4,256,128]{2,1,0:T(8,128)S(1)} collective-permute-done((f32[4,256,128]{2,1,0:T(8,128)S(1)}, f32[4,256,128]{2,1,0:T(8,128)S(1)}, u32[]{:S(2)}, u32[]{:S(2)}) %collective-permute-start.20) | collective-permute-done | bytes 524320 | tf_op jit(solution)/shard_map/ppermute | solution.py:164
  212.2 2.1 collective-permute-done.22
  214.3 0.7 collective-permute-done.21
  215.1 0.1 fusion.10
  215.2 0.7 slice_bitcast_fusion.16
  215.9 1.1 collective-permute-start.24
  217.0 2.1 collective-permute-start.23
  219.1 4.3 %collective-permute-done.25.p3_ref = f32[256,128]{1,0:T(8,128)S(1)} collective-permute-done((f32[256,128]{1,0:T(8,128)S(1)}, f32[256,128]{1,0:T(8,128)S(1)}, u32[]{:S(2)}, u32[]{:S(2)}) %collective-permute-start.25) | collective-permute-done | bytes 131104 | tf_op jit(solution)/shard_map/ppermute | solution.py:164
  223.5 0.9 collective-permute-done.23.p1_ref
  224.4 0.7 copy-done.8
  225.0 2.2 shard_map.56
  (44 shorter events, 0.8 us)
Async XLA Ops:
  0.9 2.8 %copy-start.9 = (s32[1,8,2]{1,2,0:T(2,128)S(1)}, s32[1,8,2]{1,2,0:T(2,128)}, u32[]{:S(2)}) copy-start(s32[1,8,2]{1,2,0:T(2,128)} %param.7) | copy-start | bytes 196
  2.7 23.3 %copy-start.2 = (f32[2048,256]{1,0:T(8,128)}, f32[2048,256]{1,0:T(8,128)S(1)}, u32[]{:S(2)}) copy-start(f32[2048,256]{1,0:T(8,128)S(1)} %bitcast_multiply_fusion) | copy-start | bytes 6291460
  3.5 26.1 %collective-permute-start = (f32[2048,256]{1,0:T(8,128)S(1)}, f32[2048,256]{1,0:T(8,128)}, u32[]{:S(2)}, u32[]{:S(2)}) collective-permute-start(f32[2048,256]{1,0:T(8,128)S(1)} %bitcast_multiply_fusion), channel_id=1, source_target_pairs={{0,1},{1,2},{2,3},{3,0},{64,67},{65,64},{66,65},{67,66},{4,5},{5,6... | collective-permute-start | bytes 6291464 | tf_op jit(solution)/shard_map/ppermute | solution.py:210
  29.6 42.6 %collective-permute-start.1 = (f32[2048,256]{1,0:T(8,128)}, f32[2048,256]{1,0:T(8,128)S(1)}, u32[]{:S(2)}, u32[]{:S(2)}) collective-permute-start(f32[2048,256]{1,0:T(8,128)} %collective-permute-done), channel_id=1, source_target_pairs={{0,1},{1,2},{2,3},{3,0},{64,67},{65,64},{66,65},{67,66},{4,5},{5,6... | collective-permute-start | bytes 6291464 | tf_op jit(solution)/shard_map/ppermute | solution.py:215
  72.2 6.9 %copy-start.3 = (f32[64,32,128]{2,1,0:T(8,128)}, f32[64,32,128]{2,1,0:T(8,128)S(1)}, u32[]{:S(2)}) copy-start(f32[64,32,128]{2,1,0:T(8,128)S(1)} %all_to_all.11) | copy-start | bytes 3145732
  72.2 6.9 %copy-start.4 = (f32[2048,256]{1,0:T(8,128)}, f32[2048,256]{1,0:T(8,128)S(1)}, u32[]{:S(2)}) copy-start(f32[2048,256]{1,0:T(8,128)S(1)} %collective-permute-done.1) | copy-start | bytes 6291460
  72.2 9.5 %collective-permute-start.3 = (f32[64,32,128]{2,1,0:T(8,128)S(1)}, f32[64,32,128]{2,1,0:T(8,128)}, u32[]{:S(2)}, u32[]{:S(2)}) collective-permute-start(f32[64,32,128]{2,1,0:T(8,128)S(1)} %all_to_all.11), channel_id=1, source_target_pairs={{0,64},{64,0},{1,65},{65,1},{2,66},{66,2},{3,67},{67,3},{4,68},{68... | collective-permute-start | bytes 3145736 | tf_op jit(solution)/shard_map/ppermute | solution.py:156
  72.3 25.7 %collective-permute-start.2 = (f32[64,32,128]{2,1,0:T(8,128)S(1)}, f32[64,32,128]{2,1,0:T(8,128)}, u32[]{:S(2)}, u32[]{:S(2)}) collective-permute-start(f32[64,32,128]{2,1,0:T(8,128)S(1)} %all_to_all.11), channel_id=1, source_target_pairs={{0,128},{128,0},{1,129},{129,1},{2,130},{130,2},{3,131},{131,3},{4... | collective-permute-start | bytes 3145736 | tf_op jit(solution)/shard_map/ppermute | solution.py:156
  73.0 26.1 %collective-permute-start.5 = (f32[2048,256]{1,0:T(8,128)S(1)}, f32[2048,256]{1,0:T(8,128)}, u32[]{:S(2)}, u32[]{:S(2)}) collective-permute-start(f32[2048,256]{1,0:T(8,128)S(1)} %collective-permute-done.1), channel_id=1, source_target_pairs={{0,1},{1,2},{2,3},{3,0},{64,67},{65,64},{66,65},{67,66},{4,5},{5,6... | collective-permute-start | bytes 6291464 | tf_op jit(solution)/shard_map/ppermute | solution.py:218
  98.0 3.8 %collective-permute-start.4 = (f32[64,32,128]{2,1,0:T(8,128)}, f32[64,32,128]{2,1,0:T(8,128)S(1)}, u32[]{:S(2)}, u32[]{:S(2)}) collective-permute-start(f32[64,32,128]{2,1,0:T(8,128)} %collective-permute-done.2), channel_id=1, source_target_pairs={{0,64},{64,0},{1,65},{65,1},{2,66},{66,2},{3,67},{67,3},{4,68},{68... | collective-permute-start | bytes 3145736 | tf_op jit(solution)/shard_map/ppermute | solution.py:156
  101.8 1.0 copy-start.5
  117.8 15.1 %collective-permute-start.12 = (f32[2,256,128]{2,1,0:T(8,128)S(1)}, f32[2,256,128]{2,1,0:T(8,128)S(1)}, u32[]{:S(2)}, u32[]{:S(2)}) collective-permute-start(f32[2,256,128]{2,1,0:T(8,128)S(1)} %get-tuple-element.105), channel_id=1, source_target_pairs={{0,8},{8,16},{16,24},{24,32},{32,40},{40,48},{48,56},{56,0},{1,9},... | collective-permute-start | bytes 786440 | tf_op jit(solution)/shard_map/ppermute | solution.py:164
  118.7 14.2 %collective-permute-start.6 = (f32[2,256,128]{2,1,0:T(8,128)S(1)}, f32[2,256,128]{2,1,0:T(8,128)S(1)}, u32[]{:S(2)}, u32[]{:S(2)}) collective-permute-start(f32[2,256,128]{2,1,0:T(8,128)S(1)} %get-tuple-element.108), channel_id=1, source_target_pairs={{0,8},{8,16},{16,24},{24,32},{32,40},{40,48},{48,56},{56,0},{1,9},... | collective-permute-start | bytes 786440 | tf_op jit(solution)/shard_map/ppermute | solution.py:164
  119.5 14.8 %collective-permute-start.14 = (f32[2,256,128]{2,1,0:T(8,128)S(1)}, f32[2,256,128]{2,1,0:T(8,128)S(1)}, u32[]{:S(2)}, u32[]{:S(2)}) collective-permute-start(f32[2,256,128]{2,1,0:T(8,128)S(1)} %get-tuple-element.104), channel_id=1, source_target_pairs={{0,56},{8,0},{16,8},{24,16},{32,24},{40,32},{48,40},{56,48},{1,57}... | collective-permute-start | bytes 786440 | tf_op jit(solution)/shard_map/ppermute | solution.py:164
  120.7 13.6 %collective-permute-start.9 = (f32[2,256,128]{2,1,0:T(8,128)S(1)}, f32[2,256,128]{2,1,0:T(8,128)S(1)}, u32[]{:S(2)}, u32[]{:S(2)}) collective-permute-start(f32[2,256,128]{2,1,0:T(8,128)S(1)} %get-tuple-element.106), channel_id=1, source_target_pairs={{0,56},{8,0},{16,8},{24,16},{32,24},{40,32},{48,40},{56,48},{1,57}... | collective-permute-start | bytes 786440 | tf_op jit(solution)/shard_map/ppermute | solution.py:164
  134.1 18.6 %collective-permute-start.7 = (f32[4,256,128]{2,1,0:T(8,128)S(1)}, f32[4,256,128]{2,1,0:T(8,128)S(1)}, u32[]{:S(2)}, u32[]{:S(2)}) collective-permute-start(f32[4,256,128]{2,1,0:T(8,128)S(1)} %pad_maximum_fusion), channel_id=1, source_target_pairs={{0,8},{8,16},{16,24},{24,32},{32,40},{40,48},{48,56},{56,0},{1,9},... | collective-permute-start | bytes 1572872 | tf_op jit(solution)/shard_map/ppermute | solution.py:164
  135.5 17.4 %collective-permute-start.10 = (f32[4,256,128]{2,1,0:T(8,128)S(1)}, f32[4,256,128]{2,1,0:T(8,128)S(1)}, u32[]{:S(2)}, u32[]{:S(2)}) collective-permute-start(f32[4,256,128]{2,1,0:T(8,128)S(1)} %pad_maximum_fusion.1), channel_id=1, source_target_pairs={{0,56},{8,0},{16,8},{24,16},{32,24},{40,32},{48,40},{56,48},{1,57}... | collective-permute-start | bytes 1572872 | tf_op jit(solution)/shard_map/ppermute | solution.py:164
  150.1 2.6 %copy-start.1 = (f32[2,2,4,256,128]{4,3,2,1,0:T(8,128)S(1)}, f32[2,2,4,256,128]{4,3,2,1,0:T(8,128)}, u32[]{:S(2)}) copy-start(f32[2,2,4,256,128]{4,3,2,1,0:T(8,128)} %shard_map.54) | copy-start | bytes 6291460
  150.1 14.9 %collective-permute-start.15 = (f32[4,256,128]{2,1,0:T(8,128)S(1)}, f32[4,256,128]{2,1,0:T(8,128)S(1)}, u32[]{:S(2)}, u32[]{:S(2)}) collective-permute-start(f32[4,256,128]{2,1,0:T(8,128)S(1)} %pad_maximum_fusion.3), channel_id=1, source_target_pairs={{0,56},{8,0},{16,8},{24,16},{32,24},{40,32},{48,40},{56,48},{1,57}... | collective-permute-start | bytes 1572872 | tf_op jit(solution)/shard_map/ppermute | solution.py:164
  152.6 23.8 %copy-start = (f32[4,2,4,256,128]{4,3,2,1,0:T(8,128)S(1)}, f32[4,2,4,256,128]{4,3,2,1,0:T(8,128)}, u32[]{:S(2)}) copy-start(f32[4,2,4,256,128]{4,3,2,1,0:T(8,128)} %shard_map.55) | copy-start | bytes 12582916
  152.6 14.9 %collective-permute-start.13 = (f32[4,256,128]{2,1,0:T(8,128)S(1)}, f32[4,256,128]{2,1,0:T(8,128)S(1)}, u32[]{:S(2)}, u32[]{:S(2)}) collective-permute-start(f32[4,256,128]{2,1,0:T(8,128)S(1)} %pad_maximum_fusion.2), channel_id=1, source_target_pairs={{0,8},{8,16},{16,24},{24,32},{32,40},{40,48},{48,56},{56,0},{1,9},... | collective-permute-start | bytes 1572872 | tf_op jit(solution)/shard_map/ppermute | solution.py:164
  152.8 23.5 %collective-permute-start.8 = (f32[4,256,128]{2,1,0:T(8,128)S(1)}, f32[4,256,128]{2,1,0:T(8,128)S(1)}, u32[]{:S(2)}, u32[]{:S(2)}) collective-permute-start(f32[4,256,128]{2,1,0:T(8,128)S(1)} %bitcast_add_fusion.1), channel_id=1, source_target_pairs={{0,8},{8,16},{16,24},{24,32},{32,40},{40,48},{48,56},{56,0},{1,9},... | collective-permute-start | bytes 1572872 | tf_op jit(solution)/shard_map/ppermute | solution.py:164
  154.1 22.2 %collective-permute-start.11 = (f32[4,256,128]{2,1,0:T(8,128)S(1)}, f32[4,256,128]{2,1,0:T(8,128)S(1)}, u32[]{:S(2)}, u32[]{:S(2)}) collective-permute-start(f32[4,256,128]{2,1,0:T(8,128)S(1)} %fusion.5), channel_id=1, source_target_pairs={{0,56},{8,0},{16,8},{24,16},{32,24},{40,32},{48,40},{56,48},{1,57}... | collective-permute-start | bytes 1572872 | tf_op jit(solution)/shard_map/ppermute | solution.py:164
  176.6 14.9 %collective-permute-start.19 = (f32[4,256,128]{2,1,0:T(8,128)S(1)}, f32[4,256,128]{2,1,0:T(8,128)S(1)}, u32[]{:S(2)}, u32[]{:S(2)}) collective-permute-start(f32[4,256,128]{2,1,0:T(8,128)S(1)} %get-tuple-element.100), channel_id=1, source_target_pairs={{0,56},{8,0},{16,8},{24,16},{32,24},{40,32},{48,40},{56,48},{1,57}... | collective-permute-start | bytes 1572872 | tf_op jit(solution)/shard_map/ppermute | solution.py:164
  178.2 21.2 %collective-permute-start.17 = (f32[4,256,128]{2,1,0:T(8,128)S(1)}, f32[4,256,128]{2,1,0:T(8,128)S(1)}, u32[]{:S(2)}, u32[]{:S(2)}) collective-permute-start(f32[4,256,128]{2,1,0:T(8,128)S(1)} %get-tuple-element.101), channel_id=1, source_target_pairs={{0,56},{8,0},{16,8},{24,16},{32,24},{40,32},{48,40},{56,48},{1,57}... | collective-permute-start | bytes 1572872 | tf_op jit(solution)/shard_map/ppermute | solution.py:164
  178.3 21.0 %collective-permute-start.16 = (f32[4,256,128]{2,1,0:T(8,128)S(1)}, f32[4,256,128]{2,1,0:T(8,128)S(1)}, u32[]{:S(2)}, u32[]{:S(2)}) collective-permute-start(f32[4,256,128]{2,1,0:T(8,128)S(1)} %get-tuple-element.102), channel_id=1, source_target_pairs={{0,8},{8,16},{16,24},{24,32},{32,40},{40,48},{48,56},{56,0},{1,9},... | collective-permute-start | bytes 1572872 | tf_op jit(solution)/shard_map/ppermute | solution.py:164
  180.2 21.2 %collective-permute-start.18 = (f32[4,256,128]{2,1,0:T(8,128)S(1)}, f32[4,256,128]{2,1,0:T(8,128)S(1)}, u32[]{:S(2)}, u32[]{:S(2)}) collective-permute-start(f32[4,256,128]{2,1,0:T(8,128)S(1)} %bitcast_add_fusion), channel_id=1, source_target_pairs={{0,8},{8,16},{16,24},{24,32},{32,40},{40,48},{48,56},{56,0},{1,9},... | collective-permute-start | bytes 1572872 | tf_op jit(solution)/shard_map/ppermute | solution.py:164
  201.6 10.7 %collective-permute-start.20 = (f32[4,256,128]{2,1,0:T(8,128)S(1)}, f32[4,256,128]{2,1,0:T(8,128)S(1)}, u32[]{:S(2)}, u32[]{:S(2)}) collective-permute-start(f32[4,256,128]{2,1,0:T(8,128)S(1)} %get-tuple-element.97), channel_id=1, source_target_pairs={{0,8},{8,16},{16,24},{24,32},{32,40},{40,48},{48,56},{56,0},{1,9},... | collective-permute-start | bytes 1572872 | tf_op jit(solution)/shard_map/ppermute | solution.py:164
  203.5 10.8 %collective-permute-start.22 = (f32[4,256,128]{2,1,0:T(8,128)S(1)}, f32[4,256,128]{2,1,0:T(8,128)S(1)}, u32[]{:S(2)}, u32[]{:S(2)}) collective-permute-start(f32[4,256,128]{2,1,0:T(8,128)S(1)} %get-tuple-element.98), channel_id=1, source_target_pairs={{0,4},{4,0},{1,5},{5,1},{2,6},{6,2},{3,7},{7,3},{8,12},{12,8},{9,1... | collective-permute-start | bytes 1572872 | tf_op jit(solution)/shard_map/ppermute | solution.py:156
  205.9 9.2 %collective-permute-start.21 = (f32[4,256,128]{2,1,0:T(8,128)S(1)}, f32[4,256,128]{2,1,0:T(8,128)S(1)}, u32[]{:S(2)}, u32[]{:S(2)}) collective-permute-start(f32[4,256,128]{2,1,0:T(8,128)S(1)} %get-tuple-element.99), channel_id=1, source_target_pairs={{0,56},{8,0},{16,8},{24,16},{32,24},{40,32},{48,40},{56,48},{1,57}... | collective-permute-start | bytes 1572872 | tf_op jit(solution)/shard_map/ppermute | solution.py:164
  215.9 7.6 %collective-permute-start.25 = (f32[256,128]{1,0:T(8,128)S(1)}, f32[256,128]{1,0:T(8,128)S(1)}, u32[]{:S(2)}, u32[]{:S(2)}) collective-permute-start(f32[256,128]{1,0:T(8,128)S(1)} %get-tuple-element.115), channel_id=1, source_target_pairs={{0,3},{1,0},{2,1},{3,2},{4,7},{5,4},{6,5},{7,6},{8,11},{9,8},{10,9... | collective-permute-start | bytes 393224 | tf_op jit(solution)/shard_map/ppermute | solution.py:164
  215.9 7.6 %collective-permute-start.24 = (f32[256,128]{1,0:T(8,128)S(1)}, f32[256,128]{1,0:T(8,128)S(1)}, u32[]{:S(2)}, u32[]{:S(2)}) collective-permute-start(f32[256,128]{1,0:T(8,128)S(1)} %get-tuple-element.116), channel_id=1, source_target_pairs={{0,2},{1,3},{2,0},{3,1},{4,6},{5,7},{6,4},{7,5},{8,10},{9,11},{10,... | collective-permute-start | bytes 393224 | tf_op jit(solution)/shard_map/ppermute | solution.py:164
  217.0 7.3 %collective-permute-start.23 = (f32[256,128]{1,0:T(8,128)S(1)}, f32[256,128]{1,0:T(8,128)S(1)}, u32[]{:S(2)}, u32[]{:S(2)}) collective-permute-start(f32[256,128]{1,0:T(8,128)S(1)} %get-tuple-element.117), channel_id=1, source_target_pairs={{0,1},{1,2},{2,3},{3,0},{4,5},{5,6},{6,7},{7,4},{8,9},{9,10},{10,1... | collective-permute-start | bytes 393224 | tf_op jit(solution)/shard_map/ppermute | solution.py:164
  223.5 0.9 copy-start.6
  223.5 0.9 copy-start.7
  224.4 0.7 copy-start.8

commit v4 on v3

--- a/solution.py
+++ b/solution.py
@@ -8,34 +8,38 @@
 BS = 128
 F32 = jnp.float32
 BF16 = jnp.bfloat16
-VMEM_BYTES = 56 * 1024 * 1024
+VMEM_BYTES = 20 * 1024 * 1024
 
 
 LIGHT = pl.CostEstimate(flops=1, bytes_accessed=1, transcendentals=0)
 
 
 def mask_right_kernel(pattern_ref, values_ref, out_ref):
-    at = pl.program_id(0)
-    for h in range(4):
-        for j in range(2):
-            keep = pattern_ref[(2 * at + h // 2) * 2 + j].astype(F32)
-            for i in range(2):
-                columns = slice(j * BS + i * 64, j * BS + i * 64 + 64)
-                top = values_ref[h * 64 : h * 64 + 32, columns]
-                bottom = values_ref[h * 64 + 32 : h * 64 + 64, columns]
-                out_ref[h, 0, 2 * j + i] = jnp.concatenate([top, bottom], axis=1) * keep
+    for g in range(2):
+        at = 2 * pl.program_id(0) + g
+        for h in range(4):
+            start = g * 256 + h * 64
+            for j in range(2):
+                keep = pattern_ref[(2 * at + h // 2) * 2 + j].astype(F32)
+                columns = slice(j * BS, (j + 1) * BS)
+                top = values_ref[start : start + 32, columns] * keep
+                bottom = values_ref[start + 32 : start + 64, columns] * keep
+                for i in range(2):
+                    lanes = slice(i * 64, i * 64 + 64)
+                    out_ref[h, g, 2 * j + i] = jnp.concatenate([top[:, lanes], bottom[:, lanes]], axis=1)
 
 
 def mask_right(values, pattern):
     return pl.pallas_call(
         mask_right_kernel,
-        grid=(4,),
+        grid=(2,),
         in_specs=[
             pl.BlockSpec(memory_space=pltpu.SMEM),
-            pl.BlockSpec((256, 256), lambda i: (i, 0)),
+            pl.BlockSpec((512, 256), lambda i: (i, 0)),
         ],
-        out_specs=pl.BlockSpec((4, 1, 4, 32, 128), lambda i: (0, i, 0, 0, 0)),
+        out_specs=pl.BlockSpec((4, 2, 4, 32, 128), lambda i: (0, i, 0, 0, 0)),
         out_shape=jax.ShapeDtypeStruct((4, 4, 4, 32, 128), F32),
+        compiler_params=pltpu.CompilerParams(vmem_limit_bytes=VMEM_BYTES),
         cost_estimate=LIGHT,
     )(pattern.reshape(16), values)
 
@@ -47,31 +51,32 @@
 
 def prepare_kernel(where_ref, b0_ref, b1_ref, high_ref, low_ref):
     core, xh, z = where_ref[4], where_ref[6], where_ref[7]
-    for i, ref in enumerate((b0_ref, b1_ref)):
-        base = lax.bitwise_xor(core, jnp.int32(i)) * 64
-        for near in range(2):
-            nx = lax.bitwise_xor(xh, jnp.int32(near))
-            for pair in range(4):
-                even = ref[lax.bitwise_and(z + 2 * pair, 7), nx, 0]
-                odd = ref[lax.bitwise_and(z + 2 * pair + 1, 7), nx, 0]
-                columns = slice(pair * 256 + near * 128, pair * 256 + near * 128 + 128)
-                for half in range(2):
-                    lanes = slice(half * 64, half * 64 + 64)
-                    high, low = split(jnp.concatenate([even[:, lanes], odd[:, lanes]], axis=1))
-                    rows = pl.ds(pl.multiple_of(base + half * 32, 32), 32)
+    for t in range(4):
+        ky = where_ref[t]
+        for i, ref in enumerate((b0_ref, b1_ref)):
+            base = t * BS + lax.bitwise_xor(core, jnp.int32(i)) * 64
+            rows = pl.ds(pl.multiple_of(base, 64), 64)
+            for near in range(2):
+                nx = lax.bitwise_xor(xh, jnp.int32(near))
+                for pair in range(4):
+                    even = ref[lax.bitwise_and(z + 2 * pair, 7), nx, ky]
+                    odd = ref[lax.bitwise_and(z + 2 * pair + 1, 7), nx, ky]
+                    top = jnp.concatenate([even[:, :64], odd[:, :64]], axis=1)
+                    bottom = jnp.concatenate([even[:, 64:], odd[:, 64:]], axis=1)
+                    columns = slice(pair * 256 + near * 128, pair * 256 + near * 128 + 128)
+                    high, low = split(jnp.concatenate([top, bottom], axis=0))
                     high_ref[rows, columns] = high
                     low_ref[rows, columns] = low
 
 
 def prepare(where, mine, other):
-    spec = pl.BlockSpec((8, 2, 1, 32, 128), lambda t, s: (0, 0, s[t], 0, 0))
-    out = pl.BlockSpec((128, 1024), lambda t, s: (t, 0))
+    whole = pl.BlockSpec(memory_space=pltpu.VMEM)
     return pl.pallas_call(
         prepare_kernel,
-        grid_spec=pltpu.PrefetchScalarGridSpec(
-            num_scalar_prefetch=1, grid=(4,), in_specs=[spec] * 2, out_specs=[out] * 2
-        ),
+        in_specs=[pl.BlockSpec(memory_space=pltpu.SMEM), whole, whole],
+        out_specs=[whole] * 2,
         out_shape=[jax.ShapeDtypeStruct((512, 1024), BF16)] * 2,
+        compiler_params=pltpu.CompilerParams(vmem_limit_bytes=VMEM_BYTES),
         cost_estimate=LIGHT,
     )(where, mine.reshape(8, 2, 4, 32, 128), other.reshape(8, 2, 4, 32, 128))
 
@@ -88,16 +93,20 @@
         in_specs=[spec],
         out_specs=[spec] * 2,
         out_shape=[jax.ShapeDtypeStruct((4, 512, 256), BF16)] * 2,
+        compiler_params=pltpu.CompilerParams(vmem_limit_bytes=VMEM_BYTES),
         cost_estimate=LIGHT,
     )(block.reshape(4, 512, 256))
 
 
 def product_kernel(count, where_ref, *refs):
-    weights, blocks, out_ref = refs[: 4 * count], refs[4 * count : -1], refs[-1]
+    weights, blocks, last_ref, outs = refs[: 4 * count], refs[4 * count : 4 * count + 6], refs[4 * count + 6], refs[4 * count + 7 :]
     sides = []
     for far in range(2):
         lanes = pl.ds(pl.multiple_of(lax.bitwise_xor(where_ref[5], jnp.int32(far)) * BS, BS), BS)
-        sides.append([jnp.concatenate([ref[0, :, lanes] for ref in blocks[i::2]], axis=1) for i in range(2)])
+        last = split(last_ref[0, :, lanes])
+        sides.append(
+            [jnp.concatenate([ref[0, :, lanes] for ref in blocks[i::2]] + [last[i]], axis=1) for i in range(2)]
+        )
     for at in range(count):
         terms = jnp.zeros((512, 256), F32)
         for far, (high, low) in enumerate(sides):
@@ -108,27 +117,47 @@
         for near in range(2):
             for odd in range(2):
                 lanes = slice(near * 128 + odd * 64, near * 128 + odd * 64 + 64)
-                out_ref[2 * at + odd, near, 0] = jnp.concatenate([terms[:256, lanes], terms[256:, lanes]], axis=1)
-
-
-def partial_product(where, weights, blocks, pairs):
+                packed = jnp.concatenate([terms[:256, lanes], terms[256:, lanes]], axis=1)
+                if len(outs) == 1:
+                    outs[0][2 * at + odd, near, 0] = packed
+                elif odd == 1:
+                    outs[0][near, 0] = packed
+                else:
+                    for half in range(2):
+
+                        @pl.when(pl.program_id(0) // 2 == half)
+                        def _():
+                            outs[1 + 2 * near + half][0] = packed
+
+
+def partial_product(where, weights, blocks, last, pairs, apart=False):
     n = 2 * len(pairs)
     block = pl.BlockSpec((1, 512, 256), lambda i, s: (lax.bitwise_and(s[8] + i, 3), 0, 0))
     columns = []
     for pair in pairs:
         columns += [pl.BlockSpec((512, 256), lambda i, s, pair=pair: (0, pair))] * 4
+    if apart:
+        out_specs = [pl.BlockSpec((2, 1, 256, 128), lambda i, s: (0, i, 0, 0))]
+        out_specs += [
+            pl.BlockSpec((1, 256, 128), lambda i, s: (jnp.minimum(i, 1), 0, 0)),
+            pl.BlockSpec((1, 256, 128), lambda i, s: (jnp.maximum(i - 2, 0), 0, 0)),
+        ] * 2
+        out_shape = [jax.ShapeDtypeStruct((2, 4, 256, 128), F32)] + [jax.ShapeDtypeStruct((2, 256, 128), F32)] * 4
+    else:
+        out_specs = pl.BlockSpec((n, 2, 1, 256, 128), lambda i, s: (0, 0, i, 0, 0))
+        out_shape = jax.ShapeDtypeStruct((n, 2, 4, 256, 128), F32)
     return pl.pallas_call(
         lambda *refs: product_kernel(len(pairs), *refs),
         grid_spec=pltpu.PrefetchScalarGridSpec(
             num_scalar_prefetch=1,
             grid=(4,),
-            in_specs=columns + [block] * 8,
-            out_specs=pl.BlockSpec((n, 2, 1, 256, 128), lambda i, s: (0, 0, i, 0, 0)),
+            in_specs=columns + [block] * 7,
+            out_specs=out_specs,
         ),
-        out_shape=jax.ShapeDtypeStruct((n, 2, 4, 256, 128), F32),
-        compiler_params=pltpu.CompilerParams(vmem_limit_bytes=VMEM_BYTES),
-        cost_estimate=LIGHT,
-    )(where, *(weights * len(pairs)), *blocks)
+        out_shape=out_shape,
+        compiler_params=pltpu.CompilerParams(vmem_limit_bytes=VMEM_BYTES),
+        cost_estimate=LIGHT,
+    )(where, *(weights * len(pairs)), *blocks, last.reshape(4, 512, 256))
 
 
 def assemble_kernel(where_ref, p0_ref, p1_ref, p2_ref, p3_ref, out_ref, held):
@@ -174,7 +203,7 @@
 
 def sum_over_z(ahead, behind):
     def first(own):
-        return send_both(own(4)[:2], own(4)[2:])
+        return send_both(*own(4))
 
     def second(own, right, left):
         return send_both(
@@ -221,15 +250,14 @@
     weights = prepare(where, right, swap(right, "core"))
     halves = [half for block in blocks[:3] for half in split_block(block)]
     right_far, weights, halves = tie(right_far, weights, halves)
-    halves += split_block(blocks[3])
     weights = (*weights, *prepare(where, right_far, swap(right_far, "core")))
 
-    middle = partial_product(where, weights, halves, (2,))
-    weights, middle = tie(weights, middle)
-    third = partial_product(where, weights, halves, (1,))
+    fifth, *fourth = partial_product(where, weights, halves, left3, (2,), True)
+    weights, fifth = tie(weights, fifth)
+    third = partial_product(where, weights, halves, left3, (1,))
     weights, third = tie(weights, third)
-    others = partial_product(where, weights, halves, (0, 3))
-    chunks = [others[0], others[1], third[0], third[1], middle[0], middle[1], others[2], others[3]]
+    others = partial_product(where, weights, halves, left3, (0, 3))
+    chunks = [others[0], others[1], third[0], third[1], (fourth[:2], fourth[2:]), fifth, others[2], others[3]]
     mine = sum_over_z(lambda k: chunks[k][1], lambda k: chunks[k][0])
     pieces = [mine[0]] + [shift(mine[t], "y", 4, t) for t in (1, 2, 3)]
     return assemble(where, pieces)

time: 231 us -> 215 us (0.931)
  Pallas kernels: 56.1 us -> 28.5 us
  waiting for transfers between devices: 71.4 us -> 91.4 us
  local copies, waits for them, and re-layouts: 6.53 us -> 1.85 us
  other arithmetic: 6.63 us -> 3.45 us
    ppermute x4, waiting for transfers between devices: 13.5 us -> 24.6 us  [swap(): return lax.ppermute(value, axis, [(0, 1), (1, 0)])]
    pallas_call x3, Pallas kernels: 13.3 us -> 3.4 us  [the longest x2 2.37 us: prepare(): pl.pallas_call(prepare_kernel, in_specs=[pl.BlockSpec(memory_space=pltpu....]
    pallas_call x3, Pallas kernels: 29.9 us -> 20.3 us  [partial_product(): pl.pallas_call(lambda *refs: product_kernel(len(pairs), *refs), grid_spec...]
    pallas_call x4 -> x3, Pallas kernels: 10.6 us -> 2.57 us  [split_block(): pl.pallas_call(split_kernel, grid=(2,), in_specs=[spec], out_specs=[spec]...]
    ppermute x19, waiting for transfers between devices: 53.1 us -> 59 us  [shift(): lax.ppermute(value, axis, [(i, (i + step) % size) for i in range(size)])]
    ppermute x1, waiting for transfers between devices: 3.66 us -> 7.68 us  [body(): left1 = lax.ppermute(left, ('core', 'y'), ring)]
  transfers between devices with their start and end apart: 26 -> 26, of which waited for: 14 -> 14; matrix products, arithmetic and copies ran while one was open for 2% -> 0% of each run, Pallas kernels for 18% -> 10%
where the time goes in v4:
time: 215 us; the launch traced here: 211 us
  waiting for transfers between devices  91.4 us (43%)
  blocking collectives  58.2 us (27%)
  Pallas kernels  28.5 us (13%)
  starting transfers between devices  27.8 us (13%)
  other arithmetic  3.45 us (2%)
    ppermute x19, waiting for transfers between devices, shift(): lax.ppermute(value, axis, [(i, (i + step) % size) for i in range(size)])  59 us
    all_to_all x2, blocking collectives, to_all(): return lax.all_to_all(value, axis, split_axis=0, concat_axis=0, tiled=True)  58.2 us
    ppermute x4, waiting for transfers between devices, swap(): return lax.ppermute(value, axis, [(0, 1), (1, 0)])  24.6 us
    ppermute x19, starting transfers between devices, shift(): lax.ppermute(value, axis, [(i, (i + step) % size) for i in range(size)])  22.8 us
    pallas_call x3, Pallas kernels, partial_product(): pl.pallas_call(lambda *refs: product_kernel(len(pairs), *refs), grid_spec...  20.3 us
    ppermute x1, waiting for transfers between devices, body(): left1 = lax.ppermute(left, ('core', 'y'), ring)  7.68 us
  transfers between devices with their start and end apart: 26, of which 14 were waited for; matrix products, arithmetic and copies ran while one was open for 0% of the time, Pallas kernels for 10%

profile of v4, /device:TPU:56, one launch (start us, length us, event | category | flops | bytes accessed | tf_op | source)
XLA Modules:
  0.0 211.4 jit_solution(16461290690453986451)
XLA Ops:
  0.0 0.7 convert_bitcast_fusion
  0.7 0.1 copy.7
  0.8 0.1 broadcast_in_dim.3
  0.9 1.8 bitcast_multiply_fusion
  2.7 0.1 stack.39.where_ref.refs_0_
  2.8 0.3 collective-permute-start
  3.1 0.1 copy.8
  3.2 0.1 reshape_squeeze.7.pattern_ref
  3.3 1.0 shard_map.46
  4.3 17.0 %all_to_all.10 = f32[64,32,128]{2,1,0:T(8,128)S(1)} all-to-all(f32[64,32,128]{2,1,0:T(8,128)S(1)} %bitcast.100), channel_id=1, replica_groups=mesh['xl'=2,'core'=2,'z'=8,'xh'=2,'y'=4] {'xl','core'}, dimensions={0} | all-to-all | bytes 2097152 | tf_op jit(solution)/shard_map/all_to_all | solution.py:189
  21.4 7.7 %collective-permute-done = f32[2048,256]{1,0:T(8,128)} collective-permute-done((f32[2048,256]{1,0:T(8,128)S(1)}, f32[2048,256]{1,0:T(8,128)}, u32[]{:S(2)}, u32[]{:S(2)}) %collective-permute-start) | collective-permute-done | bytes 2097184 | tf_op jit(solution)/shard_map/ppermute | solution.py:239
  29.0 1.4 collective-permute-start.1
  30.5 41.2 %all_to_all.11 = f32[64,32,128]{2,1,0:T(8,128)S(1)} all-to-all(f32[64,32,128]{2,1,0:T(8,128)S(1)} %all_to_all.10), channel_id=1, replica_groups=mesh['xl'=2,'core'=2,'z'=8,'xh'=2,'y'=4] {'z','xh','y'}, dimensions={0} | all-to-all | bytes 2097152 | tf_op jit(solution)/shard_map/all_to_all | solution.py:189
  71.7 0.6 collective-permute-start.2
  72.2 0.8 collective-permute-start.5
  73.0 0.4 shard_map.48
  73.4 1.8 shard_map.49
  75.2 0.4 shard_map.50
  75.6 1.2 shard_map.47
  76.8 20.4 %collective-permute-done.2 = f32[64,32,128]{2,1,0:T(8,128)S(1)} collective-permute-done((f32[64,32,128]{2,1,0:T(8,128)S(1)}, f32[64,32,128]{2,1,0:T(8,128)S(1)}, u32[]{:S(2)}, u32[]{:S(2)}) %collective-permute-start.2) | collective-permute-done | bytes 1048608 | tf_op jit(solution)/shard_map/ppermute | solution.py:185
  97.2 2.7 %collective-permute-done.4 = f32[64,32,128]{2,1,0:T(8,128)S(1)} collective-permute-done((f32[64,32,128]{2,1,0:T(8,128)S(1)}, f32[64,32,128]{2,1,0:T(8,128)S(1)}, u32[]{:S(2)}, u32[]{:S(2)}) %collective-permute-start.4) | collective-permute-done | bytes 1048608 | tf_op jit(solution)/shard_map/ppermute | solution.py:185
  99.9 1.2 shard_map.51
  101.1 6.0 %shard_map.52 = (f32[2,4,256,128]{3,2,1,0:T(8,128)S(1)}, f32[2,256,128]{2,1,0:T(8,128)S(1)}, f32[2,256,128]{2,1,0:T(8,128)S(1)}, f32[2,256,128]{2,1,0:T(8,128)S(1)}, f32[2,256,128]{2,1,0:T(8,128)S(1)}) custom-call(s32[9]{0:T(128)S(1)} %stack.39.where_ref.refs_0_, bf16[512,1024]{1,0:T(8,128)(2,1)S(1)} %get-tuple-element.85.refs_1_.refs_5_, ...), custom_call_target="tpu_custom_call" | custom-call | flops 1 | bytes 1 | tf_op jit(solution)/shard_map/pallas_call | solution.py:149
  107.1 1.0 collective-permute-start.6
  108.1 1.1 collective-permute-start.9
  109.2 0.9 collective-permute-start.12
  110.1 1.3 collective-permute-start.14
  111.4 5.1 %shard_map.53 = f32[2,2,4,256,128]{4,3,2,1,0:T(8,128)S(1)} custom-call(s32[9]{0:T(128)S(1)} %stack.39.where_ref.refs_0_, bf16[512,1024]{1,0:T(8,128)(2,1)S(1)} %get-tuple-element.85.refs_1_.refs_5_, bf16[512,1024]{1,0:T(8,128)(2,1)S(1)} %get-tuple-element.86.refs_2_.refs_6_, bf16[512,1024]{1,0:T(8,128)(2,1)S(1)} %get-tuple-element.87.refs_3_.refs_7_, ...), custom_call_target="tpu_custom_call" | custom-call | flops 1 | bytes 1 | tf_op jit(solution)/shard_map/pallas_call | solution.py:149
  116.6 4.6 %collective-permute-done.12 = f32[2,256,128]{2,1,0:T(8,128)S(1)} collective-permute-done((f32[2,256,128]{2,1,0:T(8,128)S(1)}, f32[2,256,128]{2,1,0:T(8,128)S(1)}, u32[]{:S(2)}, u32[]{:S(2)}) %collective-permute-start.12) | collective-permute-done | bytes 262176 | tf_op jit(solution)/shard_map/ppermute | solution.py:193
  121.1 0.1 bitcast_add_fusion.3
  121.2 1.0 collective-permute-start.7
  122.3 1.4 collective-permute-start.10
  123.7 9.2 %shard_map.54 = f32[4,2,4,256,128]{4,3,2,1,0:T(8,128)S(1)} custom-call(s32[9]{0:T(128)S(1)} %stack.39.where_ref.refs_0_, bf16[512,1024]{1,0:T(8,128)(2,1)S(1)} %get-tuple-element.85.refs_1_.refs_5_, bf16[512,1024]{1,0:T(8,128)(2,1)S(1)} %get-tuple-element.86.refs_2_.refs_6_, bf16[512,1024]{1,0:T(8,128)(2,1)S(1)} %get-tuple-element.87.refs_3_.refs_7_, ...), custom_call_target="tpu_custom_call" | custom-call | flops 1 | bytes 1 | tf_op jit(solution)/shard_map/pallas_call | solution.py:149
  133.0 3.3 %collective-permute-start.15 = (f32[4,256,128]{2,1,0:T(8,128)S(1)}, f32[4,256,128]{2,1,0:T(8,128)S(1)}, u32[]{:S(2)}, u32[]{:S(2)}) collective-permute-start(f32[4,256,128]{2,1,0:T(8,128)S(1)} %pad_maximum_fusion.3), channel_id=1, source_target_pairs={{0,56},{8,0},{16,8},{24,16},{32,24},{40,32},{48,40},{56,48},{1,57}... | collective-permute-start | bytes 1572872 | tf_op jit(solution)/shard_map/ppermute | solution.py:193
  136.3 0.1 collective-permute-start.13
  136.4 0.1 bitcast_add_fusion.1
  136.4 0.1 collective-permute-start.8
  136.5 0.1 fusion.5
  136.6 2.6 %collective-permute-start.11 = (f32[4,256,128]{2,1,0:T(8,128)S(1)}, f32[4,256,128]{2,1,0:T(8,128)S(1)}, u32[]{:S(2)}, u32[]{:S(2)}) collective-permute-start(f32[4,256,128]{2,1,0:T(8,128)S(1)} %fusion.5), channel_id=1, source_target_pairs={{0,56},{8,0},{16,8},{24,16},{32,24},{40,32},{48,40},{56,48},{1,57}... | collective-permute-start | bytes 1572872 | tf_op jit(solution)/shard_map/ppermute | solution.py:193
  139.2 9.4 %collective-permute-done.15 = f32[4,256,128]{2,1,0:T(8,128)S(1)} collective-permute-done((f32[4,256,128]{2,1,0:T(8,128)S(1)}, f32[4,256,128]{2,1,0:T(8,128)S(1)}, u32[]{:S(2)}, u32[]{:S(2)}) %collective-permute-start.15) | collective-permute-done | bytes 524320 | tf_op jit(solution)/shard_map/ppermute | solution.py:193
  148.6 2.6 %collective-permute-done.13 = f32[4,256,128]{2,1,0:T(8,128)S(1)} collective-permute-done((f32[4,256,128]{2,1,0:T(8,128)S(1)}, f32[4,256,128]{2,1,0:T(8,128)S(1)}, u32[]{:S(2)}, u32[]{:S(2)}) %collective-permute-start.13) | collective-permute-done | bytes 524320 | tf_op jit(solution)/shard_map/ppermute | solution.py:193
  151.2 8.7 %collective-permute-done.8 = f32[4,256,128]{2,1,0:T(8,128)S(1)} collective-permute-done((f32[4,256,128]{2,1,0:T(8,128)S(1)}, f32[4,256,128]{2,1,0:T(8,128)S(1)}, u32[]{:S(2)}, u32[]{:S(2)}) %collective-permute-start.8) | collective-permute-done | bytes 524320 | tf_op jit(solution)/shard_map/ppermute | solution.py:193
  159.9 0.2 fusion.3
  160.1 1.6 collective-permute-start.19
  161.7 2.0 collective-permute-start.17
  163.8 0.5 collective-permute-start.18
  164.3 10.8 %collective-permute-done.19 = f32[4,256,128]{2,1,0:T(8,128)S(1)} collective-permute-done((f32[4,256,128]{2,1,0:T(8,128)S(1)}, f32[4,256,128]{2,1,0:T(8,128)S(1)}, u32[]{:S(2)}, u32[]{:S(2)}) %collective-permute-start.19) | collective-permute-done | bytes 524320 | tf_op jit(solution)/shard_map/ppermute | solution.py:193
  175.1 7.7 %collective-permute-done.17 = f32[4,256,128]{2,1,0:T(8,128)S(1)} collective-permute-done((f32[4,256,128]{2,1,0:T(8,128)S(1)}, f32[4,256,128]{2,1,0:T(8,128)S(1)}, u32[]{:S(2)}, u32[]{:S(2)}) %collective-permute-start.17) | collective-permute-done | bytes 524320 | tf_op jit(solution)/shard_map/ppermute | solution.py:193
  182.8 3.8 %collective-permute-done.18 = f32[4,256,128]{2,1,0:T(8,128)S(1)} collective-permute-done((f32[4,256,128]{2,1,0:T(8,128)S(1)}, f32[4,256,128]{2,1,0:T(8,128)S(1)}, u32[]{:S(2)}, u32[]{:S(2)}) %collective-permute-start.18) | collective-permute-done | bytes 524320 | tf_op jit(solution)/shard_map/ppermute | solution.py:193
  186.6 0.2 fusion.7
  186.9 0.3 collective-permute-start.20
  187.2 1.9 collective-permute-start.22
  189.1 1.7 collective-permute-start.21
  190.8 7.0 %collective-permute-done.20 = f32[4,256,128]{2,1,0:T(8,128)S(1)} collective-permute-done((f32[4,256,128]{2,1,0:T(8,128)S(1)}, f32[4,256,128]{2,1,0:T(8,128)S(1)}, u32[]{:S(2)}, u32[]{:S(2)}) %collective-permute-start.20) | collective-permute-done | bytes 524320 | tf_op jit(solution)/shard_map/ppermute | solution.py:193
  197.8 1.6 collective-permute-done.22
  199.4 0.1 fusion.10
  199.5 0.7 slice_bitcast_fusion.12
  200.2 0.8 collective-permute-start.25
  201.0 2.2 %collective-permute-start.24 = (f32[256,128]{1,0:T(8,128)S(1)}, f32[256,128]{1,0:T(8,128)S(1)}, u32[]{:S(2)}, u32[]{:S(2)}) collective-permute-start(f32[256,128]{1,0:T(8,128)S(1)} %get-tuple-element.118), channel_id=1, source_target_pairs={{0,2},{1,3},{2,0},{3,1},{4,6},{5,7},{6,4},{7,5},{8,10},{9,11},{10,... | collective-permute-start | bytes 393224 | tf_op jit(solution)/shard_map/ppermute | solution.py:193
  203.2 1.1 collective-permute-start.23
  204.2 3.5 %collective-permute-done.25.p3_ref = f32[256,128]{1,0:T(8,128)S(1)} collective-permute-done((f32[256,128]{1,0:T(8,128)S(1)}, f32[256,128]{1,0:T(8,128)S(1)}, u32[]{:S(2)}, u32[]{:S(2)}) %collective-permute-start.25) | collective-permute-done | bytes 131104 | tf_op jit(solution)/shard_map/ppermute | solution.py:193
  207.7 0.8 collective-permute-done.23.p1_ref
  208.6 0.6 copy-done.4
  209.2 2.2 %shard_map.55 = f32[512,256]{1,0:T(8,128)} custom-call(s32[9]{0:T(128)} %copy-done.1, f32[256,128]{1,0:T(8,128)} %get-tuple-element.120.p0_ref, f32[256,128]{1,0:T(8,128)} %copy-done.4, f32[256,128]{1,0:T(8,128)} %copy-done.3, f32[256,128]{1,0:T(8,128)} %copy-done.2), custom_call_target="tpu_custom_call" | custom-call | flops 1 | bytes 1 | tf_op jit(solution)/shard_map/pallas_call | solution.py:174
  (35 shorter events, 0.4 us)
Async XLA Ops:
  0.9 2.2 %copy-start.5 = (s32[1,8,2]{1,2,0:T(2,128)S(1)}, s32[1,8,2]{1,2,0:T(2,128)}, u32[]{:S(2)}) copy-start(s32[1,8,2]{1,2,0:T(2,128)} %param.7) | copy-start | bytes 196
  0.9 2.4 %copy-start = (f32[1,1024,256]{2,1,0:T(8,128)S(1)}, f32[1,1024,256]{2,1,0:T(8,128)}, u32[]{:S(2)}) copy-start(f32[1,1024,256]{2,1,0:T(8,128)} %param.6) | copy-start | bytes 3145732
  2.8 120.9 %copy-start.1 = (s32[9]{0:T(128)}, s32[9]{0:T(128)S(1)}, u32[]{:S(2)}) copy-start(s32[9]{0:T(128)S(1)} %stack.39.where_ref.refs_0_) | copy-start | bytes 112
  2.8 26.2 %collective-permute-start = (f32[2048,256]{1,0:T(8,128)S(1)}, f32[2048,256]{1,0:T(8,128)}, u32[]{:S(2)}, u32[]{:S(2)}) collective-permute-start(f32[2048,256]{1,0:T(8,128)S(1)} %bitcast_multiply_fusion), channel_id=1, source_target_pairs={{0,1},{1,2},{2,3},{3,0},{64,67},{65,64},{66,65},{67,66},{4,5},{5,6... | collective-permute-start | bytes 6291464 | tf_op jit(solution)/shard_map/ppermute | solution.py:239
  29.0 42.6 %collective-permute-start.1 = (f32[2048,256]{1,0:T(8,128)}, f32[2048,256]{1,0:T(8,128)S(1)}, u32[]{:S(2)}, u32[]{:S(2)}) collective-permute-start(f32[2048,256]{1,0:T(8,128)} %collective-permute-done), channel_id=1, source_target_pairs={{0,1},{1,2},{2,3},{3,0},{64,67},{65,64},{66,65},{67,66},{4,5},{5,6... | collective-permute-start | bytes 6291464 | tf_op jit(solution)/shard_map/ppermute | solution.py:244
  71.7 4.0 %collective-permute-start.3 = (f32[64,32,128]{2,1,0:T(8,128)S(1)}, f32[64,32,128]{2,1,0:T(8,128)S(1)}, u32[]{:S(2)}, u32[]{:S(2)}) collective-permute-start(f32[64,32,128]{2,1,0:T(8,128)S(1)} %all_to_all.11), channel_id=1, source_target_pairs={{0,64},{64,0},{1,65},{65,1},{2,66},{66,2},{3,67},{67,3},{4,68},{68... | collective-permute-start | bytes 3145736 | tf_op jit(solution)/shard_map/ppermute | solution.py:185
  71.7 25.6 %collective-permute-start.2 = (f32[64,32,128]{2,1,0:T(8,128)S(1)}, f32[64,32,128]{2,1,0:T(8,128)S(1)}, u32[]{:S(2)}, u32[]{:S(2)}) collective-permute-start(f32[64,32,128]{2,1,0:T(8,128)S(1)} %all_to_all.11), channel_id=1, source_target_pairs={{0,128},{128,0},{1,129},{129,1},{2,130},{130,2},{3,131},{131,3},{4... | collective-permute-start | bytes 3145736 | tf_op jit(solution)/shard_map/ppermute | solution.py:185
  72.2 28.8 %collective-permute-start.5 = (f32[2048,256]{1,0:T(8,128)S(1)}, f32[2048,256]{1,0:T(8,128)S(1)}, u32[]{:S(2)}, u32[]{:S(2)}) collective-permute-start(f32[2048,256]{1,0:T(8,128)S(1)} %collective-permute-done.1), channel_id=1, source_target_pairs={{0,1},{1,2},{2,3},{3,0},{64,67},{65,64},{66,65},{67,66},{4,5},{5,6... | collective-permute-start | bytes 6291464 | tf_op jit(solution)/shard_map/ppermute | solution.py:247
  97.2 2.7 %collective-permute-start.4 = (f32[64,32,128]{2,1,0:T(8,128)S(1)}, f32[64,32,128]{2,1,0:T(8,128)S(1)}, u32[]{:S(2)}, u32[]{:S(2)}) collective-permute-start(f32[64,32,128]{2,1,0:T(8,128)S(1)} %collective-permute-done.2), channel_id=1, source_target_pairs={{0,64},{64,0},{1,65},{65,1},{2,66},{66,2},{3,67},{67,3},{4,68},{68... | collective-permute-start | bytes 3145736 | tf_op jit(solution)/shard_map/ppermute | solution.py:185
  107.1 9.5 %collective-permute-start.6 = (f32[2,256,128]{2,1,0:T(8,128)S(1)}, f32[2,256,128]{2,1,0:T(8,128)S(1)}, u32[]{:S(2)}, u32[]{:S(2)}) collective-permute-start(f32[2,256,128]{2,1,0:T(8,128)S(1)} %get-tuple-element.90), channel_id=1, source_target_pairs={{0,8},{8,16},{16,24},{24,32},{32,40},{40,48},{48,56},{56,0},{1,9},... | collective-permute-start | bytes 786440 | tf_op jit(solution)/shard_map/ppermute | solution.py:193
  108.1 14.1 %collective-permute-start.9 = (f32[2,256,128]{2,1,0:T(8,128)S(1)}, f32[2,256,128]{2,1,0:T(8,128)S(1)}, u32[]{:S(2)}, u32[]{:S(2)}) collective-permute-start(f32[2,256,128]{2,1,0:T(8,128)S(1)} %get-tuple-element.92), channel_id=1, source_target_pairs={{0,56},{8,0},{16,8},{24,16},{32,24},{40,32},{48,40},{56,48},{1,57}... | collective-permute-start | bytes 786440 | tf_op jit(solution)/shard_map/ppermute | solution.py:193
  109.2 11.9 %collective-permute-start.12 = (f32[2,256,128]{2,1,0:T(8,128)S(1)}, f32[2,256,128]{2,1,0:T(8,128)S(1)}, u32[]{:S(2)}, u32[]{:S(2)}) collective-permute-start(f32[2,256,128]{2,1,0:T(8,128)S(1)} %get-tuple-element.93), channel_id=1, source_target_pairs={{0,8},{8,16},{16,24},{24,32},{32,40},{40,48},{48,56},{56,0},{1,9},... | collective-permute-start | bytes 786440 | tf_op jit(solution)/shard_map/ppermute | solution.py:193
  110.1 12.1 %collective-permute-start.14 = (f32[2,256,128]{2,1,0:T(8,128)S(1)}, f32[2,256,128]{2,1,0:T(8,128)S(1)}, u32[]{:S(2)}, u32[]{:S(2)}) collective-permute-start(f32[2,256,128]{2,1,0:T(8,128)S(1)} %get-tuple-element.94), channel_id=1, source_target_pairs={{0,56},{8,0},{16,8},{24,16},{32,24},{40,32},{48,40},{56,48},{1,57}... | collective-permute-start | bytes 786440 | tf_op jit(solution)/shard_map/ppermute | solution.py:193
  121.2 15.1 %collective-permute-start.7 = (f32[4,256,128]{2,1,0:T(8,128)S(1)}, f32[4,256,128]{2,1,0:T(8,128)S(1)}, u32[]{:S(2)}, u32[]{:S(2)}) collective-permute-start(f32[4,256,128]{2,1,0:T(8,128)S(1)} %pad_maximum_fusion), channel_id=1, source_target_pairs={{0,8},{8,16},{16,24},{24,32},{32,40},{40,48},{48,56},{56,0},{1,9},... | collective-permute-start | bytes 1572872 | tf_op jit(solution)/shard_map/ppermute | solution.py:193
  122.3 14.2 %collective-permute-start.10 = (f32[4,256,128]{2,1,0:T(8,128)S(1)}, f32[4,256,128]{2,1,0:T(8,128)S(1)}, u32[]{:S(2)}, u32[]{:S(2)}) collective-permute-start(f32[4,256,128]{2,1,0:T(8,128)S(1)} %pad_maximum_fusion.1), channel_id=1, source_target_pairs={{0,56},{8,0},{16,8},{24,16},{32,24},{40,32},{48,40},{56,48},{1,57}... | collective-permute-start | bytes 1572872 | tf_op jit(solution)/shard_map/ppermute | solution.py:193
  133.0 15.7 %collective-permute-start.15 = (f32[4,256,128]{2,1,0:T(8,128)S(1)}, f32[4,256,128]{2,1,0:T(8,128)S(1)}, u32[]{:S(2)}, u32[]{:S(2)}) collective-permute-start(f32[4,256,128]{2,1,0:T(8,128)S(1)} %pad_maximum_fusion.3), channel_id=1, source_target_pairs={{0,56},{8,0},{16,8},{24,16},{32,24},{40,32},{48,40},{56,48},{1,57}... | collective-permute-start | bytes 1572872 | tf_op jit(solution)/shard_map/ppermute | solution.py:193
  136.3 14.9 %collective-permute-start.13 = (f32[4,256,128]{2,1,0:T(8,128)S(1)}, f32[4,256,128]{2,1,0:T(8,128)S(1)}, u32[]{:S(2)}, u32[]{:S(2)}) collective-permute-start(f32[4,256,128]{2,1,0:T(8,128)S(1)} %pad_maximum_fusion.2), channel_id=1, source_target_pairs={{0,8},{8,16},{16,24},{24,32},{32,40},{40,48},{48,56},{56,0},{1,9},... | collective-permute-start | bytes 1572872 | tf_op jit(solution)/shard_map/ppermute | solution.py:193
  136.4 23.4 %collective-permute-start.8 = (f32[4,256,128]{2,1,0:T(8,128)S(1)}, f32[4,256,128]{2,1,0:T(8,128)S(1)}, u32[]{:S(2)}, u32[]{:S(2)}) collective-permute-start(f32[4,256,128]{2,1,0:T(8,128)S(1)} %bitcast_add_fusion.1), channel_id=1, source_target_pairs={{0,8},{8,16},{16,24},{24,32},{32,40},{40,48},{48,56},{56,0},{1,9},... | collective-permute-start | bytes 1572872 | tf_op jit(solution)/shard_map/ppermute | solution.py:193
  136.6 23.3 %collective-permute-start.11 = (f32[4,256,128]{2,1,0:T(8,128)S(1)}, f32[4,256,128]{2,1,0:T(8,128)S(1)}, u32[]{:S(2)}, u32[]{:S(2)}) collective-permute-start(f32[4,256,128]{2,1,0:T(8,128)S(1)} %fusion.5), channel_id=1, source_target_pairs={{0,56},{8,0},{16,8},{24,16},{32,24},{40,32},{48,40},{56,48},{1,57}... | collective-permute-start | bytes 1572872 | tf_op jit(solution)/shard_map/ppermute | solution.py:193
  160.1 14.9 %collective-permute-start.19 = (f32[4,256,128]{2,1,0:T(8,128)S(1)}, f32[4,256,128]{2,1,0:T(8,128)S(1)}, u32[]{:S(2)}, u32[]{:S(2)}) collective-permute-start(f32[4,256,128]{2,1,0:T(8,128)S(1)} %get-tuple-element.106), channel_id=1, source_target_pairs={{0,56},{8,0},{16,8},{24,16},{32,24},{40,32},{48,40},{56,48},{1,57}... | collective-permute-start | bytes 1572872 | tf_op jit(solution)/shard_map/ppermute | solution.py:193
  161.7 21.1 %collective-permute-start.17 = (f32[4,256,128]{2,1,0:T(8,128)S(1)}, f32[4,256,128]{2,1,0:T(8,128)S(1)}, u32[]{:S(2)}, u32[]{:S(2)}) collective-permute-start(f32[4,256,128]{2,1,0:T(8,128)S(1)} %get-tuple-element.107), channel_id=1, source_target_pairs={{0,56},{8,0},{16,8},{24,16},{32,24},{40,32},{48,40},{56,48},{1,57}... | collective-permute-start | bytes 1572872 | tf_op jit(solution)/shard_map/ppermute | solution.py:193
  163.8 19.0 %collective-permute-start.16 = (f32[4,256,128]{2,1,0:T(8,128)S(1)}, f32[4,256,128]{2,1,0:T(8,128)S(1)}, u32[]{:S(2)}, u32[]{:S(2)}) collective-permute-start(f32[4,256,128]{2,1,0:T(8,128)S(1)} %get-tuple-element.108), channel_id=1, source_target_pairs={{0,8},{8,16},{16,24},{24,32},{32,40},{40,48},{48,56},{56,0},{1,9},... | collective-permute-start | bytes 1572872 | tf_op jit(solution)/shard_map/ppermute | solution.py:193
  163.8 22.9 %collective-permute-start.18 = (f32[4,256,128]{2,1,0:T(8,128)S(1)}, f32[4,256,128]{2,1,0:T(8,128)S(1)}, u32[]{:S(2)}, u32[]{:S(2)}) collective-permute-start(f32[4,256,128]{2,1,0:T(8,128)S(1)} %bitcast_add_fusion), channel_id=1, source_target_pairs={{0,8},{8,16},{16,24},{24,32},{32,40},{40,48},{48,56},{56,0},{1,9},... | collective-permute-start | bytes 1572872 | tf_op jit(solution)/shard_map/ppermute | solution.py:193
  186.9 10.9 %collective-permute-start.20 = (f32[4,256,128]{2,1,0:T(8,128)S(1)}, f32[4,256,128]{2,1,0:T(8,128)S(1)}, u32[]{:S(2)}, u32[]{:S(2)}) collective-permute-start(f32[4,256,128]{2,1,0:T(8,128)S(1)} %get-tuple-element.103), channel_id=1, source_target_pairs={{0,8},{8,16},{16,24},{24,32},{32,40},{40,48},{48,56},{56,0},{1,9},... | collective-permute-start | bytes 1572872 | tf_op jit(solution)/shard_map/ppermute | solution.py:193
  187.2 12.2 %collective-permute-start.22 = (f32[4,256,128]{2,1,0:T(8,128)S(1)}, f32[4,256,128]{2,1,0:T(8,128)S(1)}, u32[]{:S(2)}, u32[]{:S(2)}) collective-permute-start(f32[4,256,128]{2,1,0:T(8,128)S(1)} %get-tuple-element.104), channel_id=1, source_target_pairs={{0,4},{4,0},{1,5},{5,1},{2,6},{6,2},{3,7},{7,3},{8,12},{12,8},{9,1... | collective-permute-start | bytes 1572872 | tf_op jit(solution)/shard_map/ppermute | solution.py:185
  189.1 10.3 %collective-permute-start.21 = (f32[4,256,128]{2,1,0:T(8,128)S(1)}, f32[4,256,128]{2,1,0:T(8,128)S(1)}, u32[]{:S(2)}, u32[]{:S(2)}) collective-permute-start(f32[4,256,128]{2,1,0:T(8,128)S(1)} %get-tuple-element.105), channel_id=1, source_target_pairs={{0,56},{8,0},{16,8},{24,16},{32,24},{40,32},{48,40},{56,48},{1,57}... | collective-permute-start | bytes 1572872 | tf_op jit(solution)/shard_map/ppermute | solution.py:193
  200.2 7.6 %collective-permute-start.25 = (f32[256,128]{1,0:T(8,128)S(1)}, f32[256,128]{1,0:T(8,128)S(1)}, u32[]{:S(2)}, u32[]{:S(2)}) collective-permute-start(f32[256,128]{1,0:T(8,128)S(1)} %get-tuple-element.117), channel_id=1, source_target_pairs={{0,3},{1,0},{2,1},{3,2},{4,7},{5,4},{6,5},{7,6},{8,11},{9,8},{10,9... | collective-permute-start | bytes 393224 | tf_op jit(solution)/shard_map/ppermute | solution.py:193
  201.0 6.7 %collective-permute-start.24 = (f32[256,128]{1,0:T(8,128)S(1)}, f32[256,128]{1,0:T(8,128)S(1)}, u32[]{:S(2)}, u32[]{:S(2)}) collective-permute-start(f32[256,128]{1,0:T(8,128)S(1)} %get-tuple-element.118), channel_id=1, source_target_pairs={{0,2},{1,3},{2,0},{3,1},{4,6},{5,7},{6,4},{7,5},{8,10},{9,11},{10,... | collective-permute-start | bytes 393224 | tf_op jit(solution)/shard_map/ppermute | solution.py:193
  203.2 5.4 %collective-permute-start.23 = (f32[256,128]{1,0:T(8,128)S(1)}, f32[256,128]{1,0:T(8,128)S(1)}, u32[]{:S(2)}, u32[]{:S(2)}) collective-permute-start(f32[256,128]{1,0:T(8,128)S(1)} %get-tuple-element.119), channel_id=1, source_target_pairs={{0,1},{1,2},{2,3},{3,0},{4,5},{5,6},{6,7},{7,4},{8,9},{9,10},{10,1... | collective-permute-start | bytes 393224 | tf_op jit(solution)/shard_map/ppermute | solution.py:193
  207.7 0.9 copy-start.2
  207.7 0.9 copy-start.3
  208.6 0.7 copy-start.4

commit v5 on v4

--- a/solution.py
+++ b/solution.py
@@ -177,6 +177,7 @@
         out_specs=pl.BlockSpec(memory_space=pltpu.VMEM),
         out_shape=jax.ShapeDtypeStruct((512, 256), F32),
         scratch_shapes=[pltpu.VMEM((4, 256, 128), F32)],
+        compiler_params=pltpu.CompilerParams(vmem_limit_bytes=VMEM_BYTES),
         cost_estimate=LIGHT,
     )(where, *pieces)
 
@@ -233,8 +234,8 @@
     where = jnp.stack([(y - turn * t + 4) % 4 for t in range(4)] + [core, xl, xh, z, y]).astype(jnp.int32)
     ring = [(c * 4 + i, c * 4 + (i + 1 - 2 * c) % 4) for c in range(2) for i in range(4)]
 
-    keep = jnp.repeat(left_pattern[0].astype(F32), BS, axis=1)
-    left = (left_values[0].reshape(16, BS, 256) * keep[:, None, :]).reshape(2048, 256)
+    left = left_values[0].reshape(16, BS, 2, BS) * left_pattern[0].astype(F32)[:, None, :, None]
+    left = left.reshape(2048, 256)
     left, right_values, where = tie(left, right_values, where)
     left1 = lax.ppermute(left, ("core", "y"), ring)
 
@@ -254,10 +255,8 @@
 
     fifth, *fourth = partial_product(where, weights, halves, left3, (2,), True)
     weights, fifth = tie(weights, fifth)
-    third = partial_product(where, weights, halves, left3, (1,))
-    weights, third = tie(weights, third)
-    others = partial_product(where, weights, halves, left3, (0, 3))
-    chunks = [others[0], others[1], third[0], third[1], (fourth[:2], fourth[2:]), fifth, others[2], others[3]]
+    others = partial_product(where, weights, halves, left3, (0, 1, 3))
+    chunks = [others[0], others[1], others[2], others[3], (fourth[:2], fourth[2:]), fifth, others[4], others[5]]
     mine = sum_over_z(lambda k: chunks[k][1], lambda k: chunks[k][0])
     pieces = [mine[0]] + [shift(mine[t], "y", 4, t) for t in (1, 2, 3)]
     return assemble(where, pieces)

time: 215 us -> 213 us (level)
  waiting for transfers between devices: 91.4 us -> 96.6 us
  starting transfers between devices: 27.8 us -> 24.2 us
    ppermute x19, waiting for transfers between devices: 59 us -> 63.8 us  [shift(): lax.ppermute(value, axis, [(i, (i + step) % size) for i in range(size)])]
    ppermute x19, starting transfers between devices: 22.8 us -> 19.8 us  [shift(): lax.ppermute(value, axis, [(i, (i + step) % size) for i in range(size)])]
    pallas_call x3 -> x2, Pallas kernels: 20.3 us -> 18.9 us  [partial_product(): pl.pallas_call(lambda *refs: product_kernel(len(pairs), *refs), grid_spec...]
  transfers between devices with their start and end apart: 26 -> 26, of which waited for: 14 -> 17; matrix products, arithmetic and copies ran while one was open for 0% -> 0% of each run, Pallas kernels for 10% -> 9%
where the time goes in v5:
time: 213 us; the launch traced here: 210 us
  waiting for transfers between devices  96.6 us (45%)
  blocking collectives  58.2 us (27%)
  Pallas kernels  26.5 us (12%)
  starting transfers between devices  24.2 us (11%)
  local copies, waits for them, and re-layouts  2.5 us (1%)
    ppermute x19, waiting for transfers between devices, shift(): lax.ppermute(value, axis, [(i, (i + step) % size) for i in range(size)])  63.8 us
    all_to_all x2, blocking collectives, to_all(): return lax.all_to_all(value, axis, split_axis=0, concat_axis=0, tiled=True)  58.2 us
    ppermute x4, waiting for transfers between devices, swap(): return lax.ppermute(value, axis, [(0, 1), (1, 0)])  25.6 us
    ppermute x19, starting transfers between devices, shift(): lax.ppermute(value, axis, [(i, (i + step) % size) for i in range(size)])  19.8 us
    pallas_call x2, Pallas kernels, partial_product(): pl.pallas_call(lambda *refs: product_kernel(len(pairs), *refs), grid_spec...  18.9 us
    ppermute x1, waiting for transfers between devices, body(): left1 = lax.ppermute(left, ('core', 'y'), ring)  7.23 us
  transfers between devices with their start and end apart: 26, of which 17 were waited for; matrix products, arithmetic and copies ran while one was open for 0% of the time, Pallas kernels for 9%

profile of v5, /device:TPU:56, one launch (start us, length us, event | category | flops | bytes accessed | tf_op | source)
XLA Modules:
  0.0 210.3 jit_solution(16442646925735546684)
XLA Ops:
  0.0 0.7 convert_bitcast_fusion
  0.7 0.1 copy.7
  0.8 0.6 mul.20
  1.4 1.0 copy-done.1
  2.4 0.3 bitcast_multiply_fusion
  2.6 0.1 stack.39.where_ref.refs_0_
  2.7 0.2 collective-permute-start
  3.1 0.1 reshape_squeeze.7.pattern_ref
  3.2 0.4 copy-done
  3.6 1.0 shard_map.46
  4.6 17.0 %all_to_all.10 = f32[64,32,128]{2,1,0:T(8,128)S(1)} all-to-all(f32[64,32,128]{2,1,0:T(8,128)S(1)} %bitcast.105), channel_id=1, replica_groups=mesh['xl'=2,'core'=2,'z'=8,'xh'=2,'y'=4] {'xl','core'}, dimensions={0} | all-to-all | bytes 2097152 | tf_op jit(solution)/shard_map/all_to_all | solution.py:190
  21.6 7.2 %collective-permute-done = f32[2048,256]{1,0:T(8,128)} collective-permute-done((f32[2048,256]{1,0:T(8,128)S(1)}, f32[2048,256]{1,0:T(8,128)}, u32[]{:S(2)}, u32[]{:S(2)}) %collective-permute-start) | collective-permute-done | bytes 2097184 | tf_op jit(solution)/shard_map/ppermute | solution.py:240
  28.9 1.4 collective-permute-start.1
  30.3 41.2 %all_to_all.11 = f32[64,32,128]{2,1,0:T(8,128)S(1)} all-to-all(f32[64,32,128]{2,1,0:T(8,128)S(1)} %all_to_all.10), channel_id=1, replica_groups=mesh['xl'=2,'core'=2,'z'=8,'xh'=2,'y'=4] {'z','xh','y'}, dimensions={0} | all-to-all | bytes 2097152 | tf_op jit(solution)/shard_map/all_to_all | solution.py:190
  71.5 0.6 collective-permute-start.2
  72.1 0.8 collective-permute-start.5
  72.8 0.4 shard_map.48
  73.2 1.8 shard_map.49
  75.0 0.4 shard_map.50
  75.4 1.2 shard_map.47
  76.6 20.4 %collective-permute-done.2 = f32[64,32,128]{2,1,0:T(8,128)S(1)} collective-permute-done((f32[64,32,128]{2,1,0:T(8,128)S(1)}, f32[64,32,128]{2,1,0:T(8,128)S(1)}, u32[]{:S(2)}, u32[]{:S(2)}) %collective-permute-start.2) | collective-permute-done | bytes 1048608 | tf_op jit(solution)/shard_map/ppermute | solution.py:186
  97.1 2.7 %collective-permute-done.4 = f32[64,32,128]{2,1,0:T(8,128)S(1)} collective-permute-done((f32[64,32,128]{2,1,0:T(8,128)S(1)}, f32[64,32,128]{2,1,0:T(8,128)S(1)}, u32[]{:S(2)}, u32[]{:S(2)}) %collective-permute-start.4) | collective-permute-done | bytes 1048608 | tf_op jit(solution)/shard_map/ppermute | solution.py:186
  99.7 1.2 shard_map.51
  100.9 6.0 %shard_map.52 = (f32[2,4,256,128]{3,2,1,0:T(8,128)S(1)}, f32[2,256,128]{2,1,0:T(8,128)S(1)}, f32[2,256,128]{2,1,0:T(8,128)S(1)}, f32[2,256,128]{2,1,0:T(8,128)S(1)}, f32[2,256,128]{2,1,0:T(8,128)S(1)}) custom-call(s32[9]{0:T(128)S(1)} %stack.39.where_ref.refs_0_, bf16[512,1024]{1,0:T(8,128)(2,1)S(1)} %get-tuple-element.76.refs_1_.refs_5_.refs_9_, ...), custom_call_target="tpu_custom_call" | custom-call | flops 1 | bytes 1 | tf_op jit(solution)/shard_map/pallas_call | solution.py:149
  107.0 1.0 collective-permute-start.14
  108.0 0.1 collective-permute-start.9
  108.1 2.0 collective-permute-start.12
  110.0 1.1 collective-permute-start.6
  111.1 12.9 %shard_map.53 = f32[6,2,4,256,128]{4,3,2,1,0:T(8,128)S(1)} custom-call(s32[9]{0:T(128)S(1)} %stack.39.where_ref.refs_0_, bf16[512,1024]{1,0:T(8,128)(2,1)S(1)} %get-tuple-element.76.refs_1_.refs_5_.refs_9_, bf16[512,1024]{1,0:T(8,128)(2,1)S(1)} %get-tuple-element.77.refs_2_.refs_6_.refs_10_, ...), custom_call_target="tpu_custom_call" | custom-call | flops 1 | bytes 1 | tf_op jit(solution)/shard_map/pallas_call | solution.py:149
  124.1 0.1 fusion.13
  124.2 2.2 %collective-permute-start.7 = (f32[4,256,128]{2,1,0:T(8,128)S(1)}, f32[4,256,128]{2,1,0:T(8,128)S(1)}, u32[]{:S(2)}, u32[]{:S(2)}) collective-permute-start(f32[4,256,128]{2,1,0:T(8,128)S(1)} %pad_maximum_fusion), channel_id=1, source_target_pairs={{0,8},{8,16},{16,24},{24,32},{32,40},{40,48},{48,56},{56,0},{1,9},... | collective-permute-start | bytes 1572872 | tf_op jit(solution)/shard_map/ppermute | solution.py:194
  126.5 0.1 collective-permute-start.10
  126.7 2.2 %collective-permute-start.15 = (f32[4,256,128]{2,1,0:T(8,128)S(1)}, f32[4,256,128]{2,1,0:T(8,128)S(1)}, u32[]{:S(2)}, u32[]{:S(2)}) collective-permute-start(f32[4,256,128]{2,1,0:T(8,128)S(1)} %pad_maximum_fusion.3), channel_id=1, source_target_pairs={{0,56},{8,0},{16,8},{24,16},{32,24},{40,32},{48,40},{56,48},{1,57}... | collective-permute-start | bytes 1572872 | tf_op jit(solution)/shard_map/ppermute | solution.py:194
  128.9 0.1 collective-permute-start.13
  129.0 10.2 %collective-permute-done.7 = f32[4,256,128]{2,1,0:T(8,128)S(1)} collective-permute-done((f32[4,256,128]{2,1,0:T(8,128)S(1)}, f32[4,256,128]{2,1,0:T(8,128)S(1)}, u32[]{:S(2)}, u32[]{:S(2)}) %collective-permute-start.7) | collective-permute-done | bytes 524320 | tf_op jit(solution)/shard_map/ppermute | solution.py:194
  139.2 2.3 %collective-permute-done.10 = f32[4,256,128]{2,1,0:T(8,128)S(1)} collective-permute-done((f32[4,256,128]{2,1,0:T(8,128)S(1)}, f32[4,256,128]{2,1,0:T(8,128)S(1)}, u32[]{:S(2)}, u32[]{:S(2)}) %collective-permute-start.10) | collective-permute-done | bytes 524320 | tf_op jit(solution)/shard_map/ppermute | solution.py:194
  141.5 0.1 fusion.6
  141.6 0.1 collective-permute-start.11
  141.7 2.0 collective-permute-start.8
  143.7 9.0 %collective-permute-done.15 = f32[4,256,128]{2,1,0:T(8,128)S(1)} collective-permute-done((f32[4,256,128]{2,1,0:T(8,128)S(1)}, f32[4,256,128]{2,1,0:T(8,128)S(1)}, u32[]{:S(2)}, u32[]{:S(2)}) %collective-permute-start.15) | collective-permute-done | bytes 524320 | tf_op jit(solution)/shard_map/ppermute | solution.py:194
  152.7 8.9 %collective-permute-done.11 = f32[4,256,128]{2,1,0:T(8,128)S(1)} collective-permute-done((f32[4,256,128]{2,1,0:T(8,128)S(1)}, f32[4,256,128]{2,1,0:T(8,128)S(1)}, u32[]{:S(2)}, u32[]{:S(2)}) %collective-permute-start.11) | collective-permute-done | bytes 524320 | tf_op jit(solution)/shard_map/ppermute | solution.py:194
  161.7 0.3 fusion.3
  161.9 0.9 collective-permute-start.16
  162.8 1.2 collective-permute-start.17
  164.0 0.8 collective-permute-start.18
  164.8 1.2 collective-permute-start.19
  166.0 10.8 %collective-permute-done.16 = f32[4,256,128]{2,1,0:T(8,128)S(1)} collective-permute-done((f32[4,256,128]{2,1,0:T(8,128)S(1)}, f32[4,256,128]{2,1,0:T(8,128)S(1)}, u32[]{:S(2)}, u32[]{:S(2)}) %collective-permute-start.16) | collective-permute-done | bytes 524320 | tf_op jit(solution)/shard_map/ppermute | solution.py:194
  176.9 0.8 collective-permute-done.17
  177.7 7.2 %collective-permute-done.18 = f32[4,256,128]{2,1,0:T(8,128)S(1)} collective-permute-done((f32[4,256,128]{2,1,0:T(8,128)S(1)}, f32[4,256,128]{2,1,0:T(8,128)S(1)}, u32[]{:S(2)}, u32[]{:S(2)}) %collective-permute-start.18) | collective-permute-done | bytes 524320 | tf_op jit(solution)/shard_map/ppermute | solution.py:194
  184.9 0.5 collective-permute-done.19
  185.4 0.2 fusion.9
  185.7 1.4 collective-permute-start.20
  187.0 0.7 collective-permute-start.21
  187.8 1.4 collective-permute-start.22
  189.2 7.1 %collective-permute-done.20 = f32[4,256,128]{2,1,0:T(8,128)S(1)} collective-permute-done((f32[4,256,128]{2,1,0:T(8,128)S(1)}, f32[4,256,128]{2,1,0:T(8,128)S(1)}, u32[]{:S(2)}, u32[]{:S(2)}) %collective-permute-start.20) | collective-permute-done | bytes 524320 | tf_op jit(solution)/shard_map/ppermute | solution.py:194
  196.2 0.7 collective-permute-done.21
  197.0 2.5 %collective-permute-done.22 = f32[4,256,128]{2,1,0:T(8,128)S(1)} collective-permute-done((f32[4,256,128]{2,1,0:T(8,128)S(1)}, f32[4,256,128]{2,1,0:T(8,128)S(1)}, u32[]{:S(2)}, u32[]{:S(2)}) %collective-permute-start.22) | collective-permute-done | bytes 524320 | tf_op jit(solution)/shard_map/ppermute | solution.py:186
  199.5 0.1 fusion.12
  199.7 1.0 collective-permute-start.23
  200.7 1.8 collective-permute-start.24
  202.5 2.2 %collective-permute-done.23.p1_ref = f32[256,128]{1,0:T(8,128)S(1)} collective-permute-done((f32[256,128]{1,0:T(8,128)S(1)}, f32[256,128]{1,0:T(8,128)S(1)}, u32[]{:S(2)}, u32[]{:S(2)}) %collective-permute-start.23) | collective-permute-done | bytes 131104 | tf_op jit(solution)/shard_map/ppermute | solution.py:194
  204.7 2.5 %collective-permute-done.24.p2_ref = f32[256,128]{1,0:T(8,128)S(1)} collective-permute-done((f32[256,128]{1,0:T(8,128)S(1)}, f32[256,128]{1,0:T(8,128)S(1)}, u32[]{:S(2)}, u32[]{:S(2)}) %collective-permute-start.24) | collective-permute-done | bytes 131104 | tf_op jit(solution)/shard_map/ppermute | solution.py:194
  207.2 1.5 collective-permute-done.25.p3_ref
  208.7 1.6 shard_map.54
  (25 shorter events, 0.5 us)
Async XLA Ops:
  0.8 1.6 copy-start.1
  2.4 0.7 copy-start.2
  2.4 1.2 copy-start
  2.7 26.2 %collective-permute-start = (f32[2048,256]{1,0:T(8,128)S(1)}, f32[2048,256]{1,0:T(8,128)}, u32[]{:S(2)}, u32[]{:S(2)}) collective-permute-start(f32[2048,256]{1,0:T(8,128)S(1)} %bitcast_multiply_fusion), channel_id=1, source_target_pairs={{0,1},{1,2},{2,3},{3,0},{64,67},{65,64},{66,65},{67,66},{4,5},{5,6... | collective-permute-start | bytes 6291464 | tf_op jit(solution)/shard_map/ppermute | solution.py:240
  28.9 42.6 %collective-permute-start.1 = (f32[2048,256]{1,0:T(8,128)}, f32[2048,256]{1,0:T(8,128)S(1)}, u32[]{:S(2)}, u32[]{:S(2)}) collective-permute-start(f32[2048,256]{1,0:T(8,128)} %collective-permute-done), channel_id=1, source_target_pairs={{0,1},{1,2},{2,3},{3,0},{64,67},{65,64},{66,65},{67,66},{4,5},{5,6... | collective-permute-start | bytes 6291464 | tf_op jit(solution)/shard_map/ppermute | solution.py:245
  71.5 4.0 %collective-permute-start.3 = (f32[64,32,128]{2,1,0:T(8,128)S(1)}, f32[64,32,128]{2,1,0:T(8,128)S(1)}, u32[]{:S(2)}, u32[]{:S(2)}) collective-permute-start(f32[64,32,128]{2,1,0:T(8,128)S(1)} %all_to_all.11), channel_id=1, source_target_pairs={{0,64},{64,0},{1,65},{65,1},{2,66},{66,2},{3,67},{67,3},{4,68},{68... | collective-permute-start | bytes 3145736 | tf_op jit(solution)/shard_map/ppermute | solution.py:186
  71.5 25.6 %collective-permute-start.2 = (f32[64,32,128]{2,1,0:T(8,128)S(1)}, f32[64,32,128]{2,1,0:T(8,128)S(1)}, u32[]{:S(2)}, u32[]{:S(2)}) collective-permute-start(f32[64,32,128]{2,1,0:T(8,128)S(1)} %all_to_all.11), channel_id=1, source_target_pairs={{0,128},{128,0},{1,129},{129,1},{2,130},{130,2},{3,131},{131,3},{4... | collective-permute-start | bytes 3145736 | tf_op jit(solution)/shard_map/ppermute | solution.py:186
  72.1 28.8 %collective-permute-start.5 = (f32[2048,256]{1,0:T(8,128)S(1)}, f32[2048,256]{1,0:T(8,128)S(1)}, u32[]{:S(2)}, u32[]{:S(2)}) collective-permute-start(f32[2048,256]{1,0:T(8,128)S(1)} %collective-permute-done.1), channel_id=1, source_target_pairs={{0,1},{1,2},{2,3},{3,0},{64,67},{65,64},{66,65},{67,66},{4,5},{5,6... | collective-permute-start | bytes 6291464 | tf_op jit(solution)/shard_map/ppermute | solution.py:248
  97.1 2.7 %collective-permute-start.4 = (f32[64,32,128]{2,1,0:T(8,128)S(1)}, f32[64,32,128]{2,1,0:T(8,128)S(1)}, u32[]{:S(2)}, u32[]{:S(2)}) collective-permute-start(f32[64,32,128]{2,1,0:T(8,128)S(1)} %collective-permute-done.2), channel_id=1, source_target_pairs={{0,64},{64,0},{1,65},{65,1},{2,66},{66,2},{3,67},{67,3},{4,68},{68... | collective-permute-start | bytes 3145736 | tf_op jit(solution)/shard_map/ppermute | solution.py:186
  107.0 19.4 %collective-permute-start.14 = (f32[2,256,128]{2,1,0:T(8,128)S(1)}, f32[2,256,128]{2,1,0:T(8,128)S(1)}, u32[]{:S(2)}, u32[]{:S(2)}) collective-permute-start(f32[2,256,128]{2,1,0:T(8,128)S(1)} %get-tuple-element.84), channel_id=1, source_target_pairs={{0,56},{8,0},{16,8},{24,16},{32,24},{40,32},{48,40},{56,48},{1,57}... | collective-permute-start | bytes 786440 | tf_op jit(solution)/shard_map/ppermute | solution.py:194
  108.0 18.4 %collective-permute-start.9 = (f32[2,256,128]{2,1,0:T(8,128)S(1)}, f32[2,256,128]{2,1,0:T(8,128)S(1)}, u32[]{:S(2)}, u32[]{:S(2)}) collective-permute-start(f32[2,256,128]{2,1,0:T(8,128)S(1)} %get-tuple-element.82), channel_id=1, source_target_pairs={{0,56},{8,0},{16,8},{24,16},{32,24},{40,32},{48,40},{56,48},{1,57}... | collective-permute-start | bytes 786440 | tf_op jit(solution)/shard_map/ppermute | solution.py:194
  108.1 16.0 %collective-permute-start.12 = (f32[2,256,128]{2,1,0:T(8,128)S(1)}, f32[2,256,128]{2,1,0:T(8,128)S(1)}, u32[]{:S(2)}, u32[]{:S(2)}) collective-permute-start(f32[2,256,128]{2,1,0:T(8,128)S(1)} %get-tuple-element.83), channel_id=1, source_target_pairs={{0,8},{8,16},{16,24},{24,32},{32,40},{40,48},{48,56},{56,0},{1,9},... | collective-permute-start | bytes 786440 | tf_op jit(solution)/shard_map/ppermute | solution.py:194
  110.0 14.1 %collective-permute-start.6 = (f32[2,256,128]{2,1,0:T(8,128)S(1)}, f32[2,256,128]{2,1,0:T(8,128)S(1)}, u32[]{:S(2)}, u32[]{:S(2)}) collective-permute-start(f32[2,256,128]{2,1,0:T(8,128)S(1)} %get-tuple-element.80), channel_id=1, source_target_pairs={{0,8},{8,16},{16,24},{24,32},{32,40},{40,48},{48,56},{56,0},{1,9},... | collective-permute-start | bytes 786440 | tf_op jit(solution)/shard_map/ppermute | solution.py:194
  124.2 14.9 %collective-permute-start.7 = (f32[4,256,128]{2,1,0:T(8,128)S(1)}, f32[4,256,128]{2,1,0:T(8,128)S(1)}, u32[]{:S(2)}, u32[]{:S(2)}) collective-permute-start(f32[4,256,128]{2,1,0:T(8,128)S(1)} %pad_maximum_fusion), channel_id=1, source_target_pairs={{0,8},{8,16},{16,24},{24,32},{32,40},{40,48},{48,56},{56,0},{1,9},... | collective-permute-start | bytes 1572872 | tf_op jit(solution)/shard_map/ppermute | solution.py:194
  126.5 14.9 %collective-permute-start.10 = (f32[4,256,128]{2,1,0:T(8,128)S(1)}, f32[4,256,128]{2,1,0:T(8,128)S(1)}, u32[]{:S(2)}, u32[]{:S(2)}) collective-permute-start(f32[4,256,128]{2,1,0:T(8,128)S(1)} %pad_maximum_fusion.1), channel_id=1, source_target_pairs={{0,56},{8,0},{16,8},{24,16},{32,24},{40,32},{48,40},{56,48},{1,57}... | collective-permute-start | bytes 1572872 | tf_op jit(solution)/shard_map/ppermute | solution.py:194
  126.7 26.0 %collective-permute-start.15 = (f32[4,256,128]{2,1,0:T(8,128)S(1)}, f32[4,256,128]{2,1,0:T(8,128)S(1)}, u32[]{:S(2)}, u32[]{:S(2)}) collective-permute-start(f32[4,256,128]{2,1,0:T(8,128)S(1)} %pad_maximum_fusion.3), channel_id=1, source_target_pairs={{0,56},{8,0},{16,8},{24,16},{32,24},{40,32},{48,40},{56,48},{1,57}... | collective-permute-start | bytes 1572872 | tf_op jit(solution)/shard_map/ppermute | solution.py:194
  128.9 23.8 %collective-permute-start.13 = (f32[4,256,128]{2,1,0:T(8,128)S(1)}, f32[4,256,128]{2,1,0:T(8,128)S(1)}, u32[]{:S(2)}, u32[]{:S(2)}) collective-permute-start(f32[4,256,128]{2,1,0:T(8,128)S(1)} %pad_maximum_fusion.2), channel_id=1, source_target_pairs={{0,8},{8,16},{16,24},{24,32},{32,40},{40,48},{48,56},{56,0},{1,9},... | collective-permute-start | bytes 1572872 | tf_op jit(solution)/shard_map/ppermute | solution.py:194
  141.6 20.0 %collective-permute-start.11 = (f32[4,256,128]{2,1,0:T(8,128)S(1)}, f32[4,256,128]{2,1,0:T(8,128)S(1)}, u32[]{:S(2)}, u32[]{:S(2)}) collective-permute-start(f32[4,256,128]{2,1,0:T(8,128)S(1)} %get-tuple-element.104), channel_id=1, source_target_pairs={{0,56},{8,0},{16,8},{24,16},{32,24},{40,32},{48,40},{56,48},{1,57}... | collective-permute-start | bytes 1572872 | tf_op jit(solution)/shard_map/ppermute | solution.py:194
  141.7 19.9 %collective-permute-start.8 = (f32[4,256,128]{2,1,0:T(8,128)S(1)}, f32[4,256,128]{2,1,0:T(8,128)S(1)}, u32[]{:S(2)}, u32[]{:S(2)}) collective-permute-start(f32[4,256,128]{2,1,0:T(8,128)S(1)} %get-tuple-element.105), channel_id=1, source_target_pairs={{0,8},{8,16},{16,24},{24,32},{32,40},{40,48},{48,56},{56,0},{1,9},... | collective-permute-start | bytes 1572872 | tf_op jit(solution)/shard_map/ppermute | solution.py:194
  161.9 14.9 %collective-permute-start.16 = (f32[4,256,128]{2,1,0:T(8,128)S(1)}, f32[4,256,128]{2,1,0:T(8,128)S(1)}, u32[]{:S(2)}, u32[]{:S(2)}) collective-permute-start(f32[4,256,128]{2,1,0:T(8,128)S(1)} %get-tuple-element.99), channel_id=1, source_target_pairs={{0,8},{8,16},{16,24},{24,32},{32,40},{40,48},{48,56},{56,0},{1,9},... | collective-permute-start | bytes 1572872 | tf_op jit(solution)/shard_map/ppermute | solution.py:194
  162.8 14.9 %collective-permute-start.17 = (f32[4,256,128]{2,1,0:T(8,128)S(1)}, f32[4,256,128]{2,1,0:T(8,128)S(1)}, u32[]{:S(2)}, u32[]{:S(2)}) collective-permute-start(f32[4,256,128]{2,1,0:T(8,128)S(1)} %get-tuple-element.98), channel_id=1, source_target_pairs={{0,56},{8,0},{16,8},{24,16},{32,24},{40,32},{48,40},{56,48},{1,57}... | collective-permute-start | bytes 1572872 | tf_op jit(solution)/shard_map/ppermute | solution.py:194
  164.0 20.9 %collective-permute-start.18 = (f32[4,256,128]{2,1,0:T(8,128)S(1)}, f32[4,256,128]{2,1,0:T(8,128)S(1)}, u32[]{:S(2)}, u32[]{:S(2)}) collective-permute-start(f32[4,256,128]{2,1,0:T(8,128)S(1)} %get-tuple-element.97), channel_id=1, source_target_pairs={{0,8},{8,16},{16,24},{24,32},{32,40},{40,48},{48,56},{56,0},{1,9},... | collective-permute-start | bytes 1572872 | tf_op jit(solution)/shard_map/ppermute | solution.py:194
  164.8 20.6 %collective-permute-start.19 = (f32[4,256,128]{2,1,0:T(8,128)S(1)}, f32[4,256,128]{2,1,0:T(8,128)S(1)}, u32[]{:S(2)}, u32[]{:S(2)}) collective-permute-start(f32[4,256,128]{2,1,0:T(8,128)S(1)} %get-tuple-element.96), channel_id=1, source_target_pairs={{0,56},{8,0},{16,8},{24,16},{32,24},{40,32},{48,40},{56,48},{1,57}... | collective-permute-start | bytes 1572872 | tf_op jit(solution)/shard_map/ppermute | solution.py:194
  185.7 10.6 %collective-permute-start.20 = (f32[4,256,128]{2,1,0:T(8,128)S(1)}, f32[4,256,128]{2,1,0:T(8,128)S(1)}, u32[]{:S(2)}, u32[]{:S(2)}) collective-permute-start(f32[4,256,128]{2,1,0:T(8,128)S(1)} %get-tuple-element.93), channel_id=1, source_target_pairs={{0,8},{8,16},{16,24},{24,32},{32,40},{40,48},{48,56},{56,0},{1,9},... | collective-permute-start | bytes 1572872 | tf_op jit(solution)/shard_map/ppermute | solution.py:194
  187.0 9.9 %collective-permute-start.21 = (f32[4,256,128]{2,1,0:T(8,128)S(1)}, f32[4,256,128]{2,1,0:T(8,128)S(1)}, u32[]{:S(2)}, u32[]{:S(2)}) collective-permute-start(f32[4,256,128]{2,1,0:T(8,128)S(1)} %get-tuple-element.95), channel_id=1, source_target_pairs={{0,56},{8,0},{16,8},{24,16},{32,24},{40,32},{48,40},{56,48},{1,57}... | collective-permute-start | bytes 1572872 | tf_op jit(solution)/shard_map/ppermute | solution.py:194
  187.8 11.8 %collective-permute-start.22 = (f32[4,256,128]{2,1,0:T(8,128)S(1)}, f32[4,256,128]{2,1,0:T(8,128)S(1)}, u32[]{:S(2)}, u32[]{:S(2)}) collective-permute-start(f32[4,256,128]{2,1,0:T(8,128)S(1)} %get-tuple-element.94), channel_id=1, source_target_pairs={{0,4},{4,0},{1,5},{5,1},{2,6},{6,2},{3,7},{7,3},{8,12},{12,8},{9,1... | collective-permute-start | bytes 1572872 | tf_op jit(solution)/shard_map/ppermute | solution.py:186
  199.7 5.0 %collective-permute-start.23 = (f32[256,128]{1,0:T(8,128)S(1)}, f32[256,128]{1,0:T(8,128)S(1)}, u32[]{:S(2)}, u32[]{:S(2)}) collective-permute-start(f32[256,128]{1,0:T(8,128)S(1)} %get-tuple-element.112), channel_id=1, source_target_pairs={{0,1},{1,2},{2,3},{3,0},{4,5},{5,6},{6,7},{7,4},{8,9},{9,10},{10,1... | collective-permute-start | bytes 393224 | tf_op jit(solution)/shard_map/ppermute | solution.py:194
  200.7 6.5 %collective-permute-start.24 = (f32[256,128]{1,0:T(8,128)S(1)}, f32[256,128]{1,0:T(8,128)S(1)}, u32[]{:S(2)}, u32[]{:S(2)}) collective-permute-start(f32[256,128]{1,0:T(8,128)S(1)} %get-tuple-element.111), channel_id=1, source_target_pairs={{0,2},{1,3},{2,0},{3,1},{4,6},{5,7},{6,4},{7,5},{8,10},{9,11},{10,... | collective-permute-start | bytes 393224 | tf_op jit(solution)/shard_map/ppermute | solution.py:194
  202.5 6.2 %collective-permute-start.25 = (f32[256,128]{1,0:T(8,128)S(1)}, f32[256,128]{1,0:T(8,128)S(1)}, u32[]{:S(2)}, u32[]{:S(2)}) collective-permute-start(f32[256,128]{1,0:T(8,128)S(1)} %get-tuple-element.110), channel_id=1, source_target_pairs={{0,3},{1,0},{2,1},{3,2},{4,7},{5,4},{6,5},{7,6},{8,11},{9,8},{10,9... | collective-permute-start | bytes 393224 | tf_op jit(solution)/shard_map/ppermute | solution.py:194
